TPU v7x, 512 devices: a whole 4x8x8 slice. The times are simulated.
512 devices in a mesh: gx: 32 (over x, z), gy: 16 (over y, core).
Axes of the slice: x: 4, y: 8, z: 8, core: 2. Of those that a mesh axis runs over, the one named last changes fastest.
Arguments:
- trajectory: float32 [4, 3, 2048, 2048], P(None, None, 'gx', 'gy'), may hold values from -4 to 4
- depth: float32 [2048, 2048], P('gx', 'gy'), may hold values from 1 to 4
- cotangent: float32 [3, 2048, 2048], P(None, 'gx', 'gy'), may hold values from -6 to 6
- line_inverse: float32 [2048, 2048], P('gx'), as said below
- column_inverse: float32 [2048, 2048], P('gy'), as said below
- gauge_owner: int32 [65536, 1], P(('gx', 'gy')), may hold values from 0 to 15; in each aligned block of 128 rows (0 to 127, 128 to 255, ...) at most 16 rows name the same one
- gauge_cell: int32 [65536], P(('gx', 'gy')), may hold values from 0 to 8191
- gauge_obs: float32 [4, 65536], P(None, ('gx', 'gy')), may hold values from -4 to 4
- gauge_weight: float32 [65536], P(('gx', 'gy')), may hold values from 0.5 to 2
Outputs:
- grad_state: float32 [3, 2048, 2048], P(None, 'gx', 'gy')
- grad_depth: float32 [2048, 2048], P('gx', 'gy')
- gauge_residual: float32 [4, 65536], P(None, ('gx', 'gy'))
Inputs may be any that keep to these rules, and one draw needn't show every extreme that they name: `gauge_owner`: among the 128 gauges of one device no owner index appears more than 16 times, and some owner appears exactly 16 times. `line_inverse`: entries are positive. `column_inverse`: entries are positive.
All inputs are finite; a program needn't handle non-finite values.
Results may differ from a plain program's by a relative error of at most 0.00007.
Values sent between devices are 32-bit elements; how exact they have to be, the bound alone decides.
A program may use at most 64 MiB of HBM per device.

v0:
```python
import jax
import jax.numpy as jnp
from jax import lax
from jax.sharding import PartitionSpec as P

mass_rate = 0.25
slope_rate = 0.3
advect_rate = 0.2
highest = lax.Precision.HIGHEST


def with_halo(cells, sides, width):
    for axis, dim in sides:
        count = lax.axis_size(axis)
        ends = count - 1
        head = lax.slice_in_dim(cells, 0, width, axis=dim)
        tail = lax.slice_in_dim(cells, cells.shape[dim] - width, cells.shape[dim], axis=dim)
        cells = jnp.concatenate(
            [
                lax.ppermute(tail, axis, [(i, (i + 1) % count) for i in range(ends)]),
                cells,
                lax.ppermute(head, axis, [((i + 1) % count, i) for i in range(ends)]),
            ],
            axis=dim,
        )
    return cells


def gradient_padded(padded, axis):
    length = padded.shape[axis] - 4

    def window(offset):
        return lax.slice_in_dim(padded, offset, offset + length, axis=axis)

    return (window(0) - 8.0 * window(1) + 8.0 * window(3) - window(4)) / 12.0


def per_device(
    trajectory,
    depth,
    cotangent,
    line_inverse,
    column_inverse,
    gauge_owner,
    gauge_cell,
    gauge_obs,
    gauge_weight,
):
    steps_count, unused, rows, cols = trajectory.shape
    owners_count = lax.axis_size("gy")
    records = gauge_cell.shape[0]
    surface_flat = trajectory[:, 0].reshape(steps_count, rows * cols)
    payload = jnp.concatenate([gauge_obs, gauge_weight[None, :]], 0)
    capacity = 2 * records // owners_count
    owner = gauge_owner[:, 0]
    member = (owner[:, None] == jnp.arange(owners_count, dtype=jnp.int32)[None, :]).astype(
        jnp.int32
    )
    ranked = jnp.sum(jnp.cumsum(member, axis=0) * member, axis=1) - 1
    target = owner * capacity + ranked
    outgoing = (
        jnp.zeros((steps_count + 1, owners_count * capacity), jnp.float32)
        .at[:, target]
        .set(payload)
    )
    places = (
        jnp.zeros((1, owners_count * capacity), jnp.int32).at[:, target].set(gauge_cell[None, :])
    )
    arrived, arrived_cells = (
        lax.all_to_all(
            outgoing.reshape(steps_count + 1, owners_count, capacity),
            "gy",
            split_axis=1,
            concat_axis=1,
            tiled=True,
        ),
        lax.all_to_all(
            places.reshape(1, owners_count, capacity), "gy", split_axis=1, concat_axis=1, tiled=True
        ),
    )
    arrived = arrived.reshape(steps_count + 1, owners_count * capacity)
    cell_list = arrived_cells.reshape(owners_count * capacity)
    misfit = surface_flat[:, cell_list] - arrived[:steps_count]
    forcing = arrived[steps_count][None, :] * misfit
    returned = lax.all_to_all(
        misfit.reshape(steps_count, owners_count, capacity),
        "gy",
        split_axis=1,
        concat_axis=1,
        tiled=True,
    )
    gauge_residual = returned.reshape(steps_count, owners_count * capacity)[:, target]
    adjoint = cotangent
    grad_depth = jnp.zeros(depth.shape, jnp.float32)
    for section in reversed(range(steps_count)):
        surface = trajectory[section, 0]
        eastward = trajectory[section, 1]
        northward = trajectory[section, 2]
        total = depth + surface
        padded = with_halo(trajectory[section, 1:3], (("gx", 1), ("gy", 2)), 2)
        slopes_x = gradient_padded(padded[:, :, 2 : 2 + cols], 1)
        slopes_y = gradient_padded(padded[:, 2 : 2 + rows, :], 2)
        back_surface, back_east, back_north = (adjoint[0], adjoint[1], adjoint[2])
        gathered = lax.all_gather(back_east, "gx", axis=0, tiled=True)
        line_adjoint = jnp.dot(line_inverse, gathered, precision=highest)
        column_adjoint = lax.dot_general(
            lax.all_gather(back_north, "gy", axis=1, tiled=True),
            column_inverse,
            (((1,), (1,)), ((), ())),
            precision=highest,
        )
        stack_x = jnp.stack(
            [back_surface, line_adjoint, eastward * line_adjoint, eastward * column_adjoint]
        )
        stack_y = jnp.stack(
            [back_surface, column_adjoint, northward * line_adjoint, northward * column_adjoint]
        )
        along_x = gradient_padded(with_halo(stack_x, (("gx", 1),), 2), 1)
        along_y = gradient_padded(with_halo(stack_y, (("gy", 2),), 2), 2)
        flux_x = mass_rate * along_x[0]
        flux_y = mass_rate * along_y[0]
        new_surface = (
            back_surface
            + slope_rate * along_x[1]
            + slope_rate * along_y[1]
            + eastward * flux_x
            + northward * flux_y
        )
        new_east = (
            line_adjoint
            - advect_rate * line_adjoint * slopes_x[0]
            + advect_rate * along_x[2]
            + advect_rate * along_y[2]
            - advect_rate * column_adjoint * slopes_x[1]
            + total * flux_x
        )
        new_north = (
            column_adjoint
            - advect_rate * line_adjoint * slopes_y[0]
            + advect_rate * along_x[3]
            - advect_rate * column_adjoint * slopes_y[1]
            + advect_rate * along_y[3]
            + total * flux_y
        )
        grad_depth = grad_depth + eastward * flux_x + northward * flux_y
        new_surface = (
            new_surface.reshape(rows * cols).at[cell_list].add(forcing[section]).reshape(rows, cols)
        )
        adjoint = jnp.stack([new_surface, new_east, new_north])
    return (adjoint, grad_depth, gauge_residual)


def solution(mesh):
    return jax.shard_map(
        per_device,
        mesh=mesh,
        in_specs=(
            P(None, None, "gx", "gy"),
            P("gx", "gy"),
            P(None, "gx", "gy"),
            P("gx", None),
            P("gy", None),
            P(("gx", "gy"), None),
            P(("gx", "gy")),
            P(None, ("gx", "gy")),
            P(("gx", "gy")),
        ),
        out_specs=(P(None, "gx", "gy"), P("gx", "gy"), P(None, ("gx", "gy"))),
        check_vma=False,
    )
```

profile of v0, /device:TPU:1, one launch (start us, length us, event | category | flops | bytes accessed | tf_op | source)
XLA Modules:
  0.0 424.1 jit_solution(12305242220442229788)
XLA Ops:
  13.0 10.1 %all-to-all-start = ((s32[1,16,16]{2,0,1:T(1,128)}), s32[1,16,16]{2,0,1:T(1,128)S(1)}, u32[]{:S(2)}, u32[]{:S(2)}) async-start(s32[1,16,16]{2,0,1:T(1,128)} %reshape.172), calls=%async_computation | async-start | bytes 16384 | tf_op jit(solution)/shard_map/all_to_all | solution.py:77
  24.0 2.7 collective-permute-start.4
  28.0 4.6 %collective-permute-start.12 = (f32[2,2,128]{2,1,0:T(2,128)S(1)}, f32[2,2,128]{2,1,0:T(2,128)S(1)}, u32[]{:S(2)}, u32[]{:S(2)}) collective-permute-start(f32[2,2,128]{2,1,0:T(2,128)S(1)} %get-tuple-element.101), channel_id=1, source_target_pairs={{0,16},{16,32},{32,48},{48,64},{64,80},{80,96},{96,112},{112,128},... | collective-permute-start | bytes 6152 | tf_op jit(solution)/shard_map/ppermute | solution.py:20
  34.0 19.2 %all-gather.1 = f32[1,64,2048]{2,1,0:T(8,128)S(1)} all-gather(f32[1,64,128]{2,1,0:T(8,128)S(1)} %get-tuple-element.86), channel_id=3, replica_groups=mesh['gx'=32,'gy'=16] {'gy'}, dimensions={2}, use_global_device_ids=true | all-gather | bytes 557056 | tf_op jit(solution)/shard_map/all_gather | solution.py:107
  56.0 2.7 copy.24
  60.5 4.7 %all-to-all-start.1 = ((f32[5,16,16]{2,0,1:T(8,128)}), f32[5,16,16]{2,0,1:T(8,128)S(1)}, u32[]{:S(2)}, u32[]{:S(2)}) async-start(f32[5,16,16]{2,0,1:T(8,128)} %copy.23), calls=%async_computation.1 | async-start | bytes 131072 | tf_op jit(solution)/shard_map/all_to_all | solution.py:70
  66.7 3.5 collective-permute-start.6
  72.2 4.1 collective-permute-done.7
  76.5 18.7 %all-gather.13.cloned.1.call-done = f32[1,2048,128]{2,1,0:T(8,128)} async-done(((f32[1,64,128]{2,1,0:T(8,128)}), f32[1,2048,128]{2,1,0:T(8,128)}) %all-gather.13.cloned.1.call-update) | async-done | bytes 1048592 | tf_op jit(solution)/shard_map/all_gather | solution.py:104
  95.2 2.0 fusion
  97.4 8.0 %collective-permute-start.2 = (f32[4,64,2]{2,1,0:T(8,128)S(1)}, f32[4,64,2]{2,1,0:T(8,128)S(1)}, u32[]{:S(2)}, u32[]{:S(2)}) collective-permute-start(f32[4,64,2]{2,1,0:T(8,128)S(1)} %get-tuple-element.82), channel_id=1, source_target_pairs={{0,1},{1,2},{2,3},{3,4},{4,5},{5,6},{6,7},{7,8},{8,9},{9,10},{10,1... | collective-permute-start | bytes 6152 | tf_op jit(solution)/shard_map/ppermute | solution.py:20
  107.3 2.4 collective-permute-start
  111.8 2.4 collective-permute-done.1
  115.2 2.9 gather_fusion
  118.4 4.9 %collective-permute-start.14 = (f32[2,68,2]{2,1,0:T(8,128)S(1)}, f32[2,68,2]{2,1,0:T(8,128)S(1)}, u32[]{:S(2)}, u32[]{:S(2)}) collective-permute-start(f32[2,68,2]{2,1,0:T(8,128)S(1)} %get-tuple-element.91), channel_id=1, source_target_pairs={{0,1},{1,2},{2,3},{3,4},{4,5},{5,6},{6,7},{7,8},{8,9},{9,10},{10,1... | collective-permute-start | bytes 3272 | tf_op jit(solution)/shard_map/ppermute | solution.py:20
  125.2 3.7 collective-permute-done.15
  131.3 2.0 scatter_fusion
  133.3 17.7 %all_gather.27 = f32[64,2048]{1,0:T(8,128)S(1)} all-gather(f32[64,128]{1,0:T(8,128)S(1)} %get-tuple-element.23), channel_id=1, replica_groups=mesh['gx'=32,'gy'=16] {'gy'}, dimensions={1}, use_global_device_ids=true | all-gather | bytes 557056 | tf_op jit(solution)/shard_map/all_gather | solution.py:107
  152.2 42.8 %all-gather.7.cloned.1.call-done = f32[2048,128]{1,0:T(8,128)} async-done(((f32[64,128]{1,0:T(8,128)}), f32[2048,128]{1,0:T(8,128)}) %all-gather.7.cloned.1.call-update) | async-done | bytes 1048592 | tf_op jit(solution)/shard_map/all_gather | solution.py:104
  195.0 2.0 fusion.239
  197.1 8.1 %collective-permute-start.10 = (f32[4,64,2]{2,1,0:T(8,128)S(1)}, f32[4,64,2]{2,1,0:T(8,128)S(1)}, u32[]{:S(2)}, u32[]{:S(2)}) collective-permute-start(f32[4,64,2]{2,1,0:T(8,128)S(1)} %get-tuple-element.74), channel_id=1, source_target_pairs={{0,1},{1,2},{2,3},{3,4},{4,5},{5,6},{6,7},{7,8},{8,9},{9,10},{10,1... | collective-permute-start | bytes 6152 | tf_op jit(solution)/shard_map/ppermute | solution.py:20
  207.2 2.4 collective-permute-start.8
  211.9 2.4 collective-permute-done.9
  215.1 3.4 collective-permute-start.20
  219.8 3.1 collective-permute-done.21
  223.0 6.4 %collective-permute-start.22 = (f32[2,68,2]{2,1,0:T(8,128)S(1)}, f32[2,68,2]{2,1,0:T(8,128)S(1)}, u32[]{:S(2)}, u32[]{:S(2)}) collective-permute-start(f32[2,68,2]{2,1,0:T(8,128)S(1)} %get-tuple-element.89), channel_id=1, source_target_pairs={{0,1},{1,2},{2,3},{3,4},{4,5},{5,6},{6,7},{7,8},{8,9},{9,10},{10,1... | collective-permute-start | bytes 3272 | tf_op jit(solution)/shard_map/ppermute | solution.py:20
  229.4 1.9 collective-permute-start.23
  231.4 3.7 collective-permute-done.23
  235.3 2.2 scatter_fusion.1
  237.5 17.5 %all_gather.29 = f32[64,2048]{1,0:T(8,128)S(1)} all-gather(f32[64,128]{1,0:T(8,128)S(1)} %get-tuple-element.21), channel_id=1, replica_groups=mesh['gx'=32,'gy'=16] {'gy'}, dimensions={1}, use_global_device_ids=true | all-gather | bytes 557056 | tf_op jit(solution)/shard_map/all_gather | solution.py:107
  256.3 38.7 %all-gather.9.cloned.1.call-done = f32[2048,128]{1,0:T(8,128)} async-done(((f32[64,128]{1,0:T(8,128)}), f32[2048,128]{1,0:T(8,128)}) %all-gather.9.cloned.1.call-update) | async-done | bytes 1048592 | tf_op jit(solution)/shard_map/all_gather | solution.py:104
  294.9 2.0 fusion.241
  297.1 8.1 %collective-permute-start.18 = (f32[4,64,2]{2,1,0:T(8,128)S(1)}, f32[4,64,2]{2,1,0:T(8,128)S(1)}, u32[]{:S(2)}, u32[]{:S(2)}) collective-permute-start(f32[4,64,2]{2,1,0:T(8,128)S(1)} %get-tuple-element.66), channel_id=1, source_target_pairs={{0,1},{1,2},{2,3},{3,4},{4,5},{5,6},{6,7},{7,8},{8,9},{9,10},{10,1... | collective-permute-start | bytes 6152 | tf_op jit(solution)/shard_map/ppermute | solution.py:20
  307.1 2.4 collective-permute-start.16
  311.8 2.4 collective-permute-done.17
  315.0 3.4 collective-permute-start.28
  319.7 3.2 collective-permute-done.29
  322.9 6.3 %collective-permute-start.30 = (f32[2,68,2]{2,1,0:T(8,128)S(1)}, f32[2,68,2]{2,1,0:T(8,128)S(1)}, u32[]{:S(2)}, u32[]{:S(2)}) collective-permute-start(f32[2,68,2]{2,1,0:T(8,128)S(1)} %get-tuple-element.87), channel_id=1, source_target_pairs={{0,1},{1,2},{2,3},{3,4},{4,5},{5,6},{6,7},{7,8},{8,9},{9,10},{10,1... | collective-permute-start | bytes 3272 | tf_op jit(solution)/shard_map/ppermute | solution.py:20
  331.2 9.8 %all-to-all-start.2 = ((f32[4,16,16]{2,0,1:T(4,128)}), f32[4,16,16]{2,0,1:T(4,128)S(1)}, u32[]{:S(2)}, u32[]{:S(2)}) async-start(f32[4,16,16]{2,0,1:T(4,128)} %get-tuple-element.95), calls=%async_computation.2 | async-start | bytes 65536 | tf_op jit(solution)/shard_map/all_to_all | solution.py:85
  341.3 7.2 %all-to-all-done.2 = f32[4,16,16]{2,0,1:T(4,128)S(1)} async-done(((f32[4,16,16]{2,0,1:T(4,128)}), f32[4,16,16]{2,0,1:T(4,128)S(1)}, u32[]{:S(2)}, u32[]{:S(2)}) %all-to-all-start.2) | async-done | bytes 4128 | tf_op jit(solution)/shard_map/all_to_all | solution.py:85
  349.9 2.0 scatter_fusion.2
  352.0 16.4 %all_gather.31 = f32[64,2048]{1,0:T(8,128)S(1)} all-gather(f32[64,128]{1,0:T(8,128)S(1)} %get-tuple-element.19), channel_id=1, replica_groups=mesh['gx'=32,'gy'=16] {'gy'}, dimensions={1}, use_global_device_ids=true | all-gather | bytes 557056 | tf_op jit(solution)/shard_map/all_gather | solution.py:107
  369.6 25.2 %all-gather.11.cloned.1.call-done = f32[2048,128]{1,0:T(8,128)} async-done(((f32[64,128]{1,0:T(8,128)}), f32[2048,128]{1,0:T(8,128)}) %all-gather.11.cloned.1.call-update) | async-done | bytes 1048592 | tf_op jit(solution)/shard_map/all_gather | solution.py:104
  394.8 2.0 fusion.243
  396.9 8.1 %collective-permute-start.26 = (f32[4,64,2]{2,1,0:T(8,128)S(1)}, f32[4,64,2]{2,1,0:T(8,128)S(1)}, u32[]{:S(2)}, u32[]{:S(2)}) collective-permute-start(f32[4,64,2]{2,1,0:T(8,128)S(1)} %get-tuple-element.58), channel_id=1, source_target_pairs={{0,1},{1,2},{2,3},{3,4},{4,5},{5,6},{6,7},{7,8},{8,9},{9,10},{10,1... | collective-permute-start | bytes 6152 | tf_op jit(solution)/shard_map/ppermute | solution.py:20
  407.0 2.4 collective-permute-start.24
  411.6 2.4 collective-permute-done.25
  414.8 2.0 scatter_fusion.3
  (150 shorter events, 53.4 us)
Async XLA Ops:
  7.2 46.0 %copy-start = (f32[128,2048]{1,0:T(8,128)S(1)}, f32[128,2048]{1,0:T(8,128)}, u32[]{:S(2)}) copy-start(f32[128,2048]{1,0:T(8,128)} %param.13) | copy-start | bytes 3145732
  7.2 88.1 %all-gather.13.cloned.1.call-start = ((), (), s32[]{:S(2)}) async-start(), calls=%async_computation.6 | async-start | bytes 1081344 | tf_op jit(solution)/shard_map/all_gather | solution.py:104
  13.0 47.6 %all-to-all-start = ((s32[1,16,16]{2,0,1:T(1,128)}), s32[1,16,16]{2,0,1:T(1,128)S(1)}, u32[]{:S(2)}, u32[]{:S(2)}) async-start(s32[1,16,16]{2,0,1:T(1,128)} %reshape.172), calls=%async_computation | async-start | bytes 16384 | tf_op jit(solution)/shard_map/all_to_all | solution.py:77
  24.0 71.3 %copy-start.1 = (f32[64,2048]{1,0:T(8,128)S(1)}, f32[64,2048]{1,0:T(8,128)}, u32[]{:S(2)}) copy-start(f32[64,2048]{1,0:T(8,128)} %param.12) | copy-start | bytes 1572868
  24.0 42.6 %collective-permute-start.4 = (f32[2,2,128]{2,1,0:T(2,128)S(1)}, f32[2,2,128]{2,1,0:T(2,128)S(1)}, u32[]{:S(2)}, u32[]{:S(2)}) collective-permute-start(f32[2,2,128]{2,1,0:T(2,128)S(1)} %get-tuple-element.103), channel_id=1, source_target_pairs={{0,16},{16,32},{32,48},{48,64},{64,80},{80,96},{96,112},{112,128},... | collective-permute-start | bytes 6152 | tf_op jit(solution)/shard_map/ppermute | solution.py:20
  26.7 39.9 %collective-permute-start.5 = (f32[2,2,128]{2,1,0:T(2,128)S(1)}, f32[2,2,128]{2,1,0:T(2,128)S(1)}, u32[]{:S(2)}, u32[]{:S(2)}) collective-permute-start(f32[2,2,128]{2,1,0:T(2,128)S(1)} %get-tuple-element.104), channel_id=1, source_target_pairs={{16,0},{32,16},{48,32},{64,48},{80,64},{96,80},{112,96},{128,112},... | collective-permute-start | bytes 6152 | tf_op jit(solution)/shard_map/ppermute | solution.py:22
  28.0 90.2 %collective-permute-start.12 = (f32[2,2,128]{2,1,0:T(2,128)S(1)}, f32[2,2,128]{2,1,0:T(2,128)S(1)}, u32[]{:S(2)}, u32[]{:S(2)}) collective-permute-start(f32[2,2,128]{2,1,0:T(2,128)S(1)} %get-tuple-element.101), channel_id=1, source_target_pairs={{0,16},{16,32},{32,48},{48,64},{64,80},{80,96},{96,112},{112,128},... | collective-permute-start | bytes 6152 | tf_op jit(solution)/shard_map/ppermute | solution.py:20
  32.7 85.6 %collective-permute-start.13 = (f32[2,2,128]{2,1,0:T(2,128)S(1)}, f32[2,2,128]{2,1,0:T(2,128)S(1)}, u32[]{:S(2)}, u32[]{:S(2)}) collective-permute-start(f32[2,2,128]{2,1,0:T(2,128)S(1)} %get-tuple-element.102), channel_id=1, source_target_pairs={{16,0},{32,16},{48,32},{64,48},{80,64},{96,80},{112,96},{128,112},... | collective-permute-start | bytes 6152 | tf_op jit(solution)/shard_map/ppermute | solution.py:22
  54.3 42.9 %copy-start.2 = (f32[4,3,64,128]{3,2,1,0:T(8,128)S(1)}, f32[4,3,64,128]{3,2,1,0:T(8,128)}, u32[]{:S(2)}) copy-start(f32[4,3,64,128]{3,2,1,0:T(8,128)} %param.9) | copy-start | bytes 1179652
  58.7 55.7 %copy-start.3 = (f32[64,128]{1,0:T(8,128)S(1)}, f32[64,128]{1,0:T(8,128)}, u32[]{:S(2)}) copy-start(f32[64,128]{1,0:T(8,128)} %param.10) | copy-start | bytes 98308
  60.5 68.6 %all-to-all-start.1 = ((f32[5,16,16]{2,0,1:T(8,128)}), f32[5,16,16]{2,0,1:T(8,128)S(1)}, u32[]{:S(2)}, u32[]{:S(2)}) async-start(f32[5,16,16]{2,0,1:T(8,128)} %copy.23), calls=%async_computation.1 | async-start | bytes 131072 | tf_op jit(solution)/shard_map/all_to_all | solution.py:70
  65.3 129.7 %all-gather.7.cloned.1.call-start = ((), (), s32[]{:S(2)}) async-start(), calls=%async_computation.3 | async-start | bytes 1081344 | tf_op jit(solution)/shard_map/all_gather | solution.py:104
  66.7 5.5 %collective-permute-start.6 = (f32[2,68,2]{2,1,0:T(8,128)S(1)}, f32[2,68,2]{2,1,0:T(8,128)S(1)}, u32[]{:S(2)}, u32[]{:S(2)}) collective-permute-start(f32[2,68,2]{2,1,0:T(8,128)S(1)} %get-tuple-element.93), channel_id=1, source_target_pairs={{0,1},{1,2},{2,3},{3,4},{4,5},{5,6},{6,7},{7,8},{8,9},{9,10},{10,1... | collective-permute-start | bytes 3272 | tf_op jit(solution)/shard_map/ppermute | solution.py:20
  70.2 6.1 %collective-permute-start.7 = (f32[2,68,2]{2,1,0:T(8,128)S(1)}, f32[2,68,2]{2,1,0:T(8,128)S(1)}, u32[]{:S(2)}, u32[]{:S(2)}) collective-permute-start(f32[2,68,2]{2,1,0:T(8,128)S(1)} %get-tuple-element.94), channel_id=1, source_target_pairs={{1,0},{2,1},{3,2},{4,3},{5,4},{6,5},{7,6},{8,7},{9,8},{10,9},{11,1... | collective-permute-start | bytes 3272 | tf_op jit(solution)/shard_map/ppermute | solution.py:22
  97.4 12.3 %collective-permute-start.2 = (f32[4,64,2]{2,1,0:T(8,128)S(1)}, f32[4,64,2]{2,1,0:T(8,128)S(1)}, u32[]{:S(2)}, u32[]{:S(2)}) collective-permute-start(f32[4,64,2]{2,1,0:T(8,128)S(1)} %get-tuple-element.82), channel_id=1, source_target_pairs={{0,1},{1,2},{2,3},{3,4},{4,5},{5,6},{6,7},{7,8},{8,9},{9,10},{10,1... | collective-permute-start | bytes 6152 | tf_op jit(solution)/shard_map/ppermute | solution.py:20
  105.4 6.3 %collective-permute-start.3 = (f32[4,64,2]{2,1,0:T(8,128)S(1)}, f32[4,64,2]{2,1,0:T(8,128)S(1)}, u32[]{:S(2)}, u32[]{:S(2)}) collective-permute-start(f32[4,64,2]{2,1,0:T(8,128)S(1)} %get-tuple-element.83), channel_id=1, source_target_pairs={{1,0},{2,1},{3,2},{4,3},{5,4},{6,5},{7,6},{8,7},{9,8},{10,9},{11,1... | collective-permute-start | bytes 6152 | tf_op jit(solution)/shard_map/ppermute | solution.py:22
  107.3 4.5 %collective-permute-start = (f32[4,2,128]{2,1,0:T(2,128)S(1)}, f32[4,2,128]{2,1,0:T(2,128)S(1)}, u32[]{:S(2)}, u32[]{:S(2)}) collective-permute-start(f32[4,2,128]{2,1,0:T(2,128)S(1)} %get-tuple-element.78), channel_id=1, source_target_pairs={{0,16},{16,32},{32,48},{48,64},{64,80},{80,96},{96,112},{112,128},... | collective-permute-start | bytes 12296 | tf_op jit(solution)/shard_map/ppermute | solution.py:20
  109.7 4.6 %collective-permute-start.1 = (f32[4,2,128]{2,1,0:T(2,128)S(1)}, f32[4,2,128]{2,1,0:T(2,128)S(1)}, u32[]{:S(2)}, u32[]{:S(2)}) collective-permute-start(f32[4,2,128]{2,1,0:T(2,128)S(1)} %get-tuple-element.79), channel_id=1, source_target_pairs={{16,0},{32,16},{48,32},{64,48},{80,64},{96,80},{112,96},{128,112},... | collective-permute-start | bytes 12296 | tf_op jit(solution)/shard_map/ppermute | solution.py:22
  115.1 179.8 %all-gather.9.cloned.1.call-start = ((), (), s32[]{:S(2)}) async-start(), calls=%async_computation.4 | async-start | bytes 1081344 | tf_op jit(solution)/shard_map/all_gather | solution.py:104
  118.4 6.9 %collective-permute-start.14 = (f32[2,68,2]{2,1,0:T(8,128)S(1)}, f32[2,68,2]{2,1,0:T(8,128)S(1)}, u32[]{:S(2)}, u32[]{:S(2)}) collective-permute-start(f32[2,68,2]{2,1,0:T(8,128)S(1)} %get-tuple-element.91), channel_id=1, source_target_pairs={{0,1},{1,2},{2,3},{3,4},{4,5},{5,6},{6,7},{7,8},{8,9},{9,10},{10,1... | collective-permute-start | bytes 3272 | tf_op jit(solution)/shard_map/ppermute | solution.py:20
  123.3 5.7 %collective-permute-start.15 = (f32[2,68,2]{2,1,0:T(8,128)S(1)}, f32[2,68,2]{2,1,0:T(8,128)S(1)}, u32[]{:S(2)}, u32[]{:S(2)}) collective-permute-start(f32[2,68,2]{2,1,0:T(8,128)S(1)} %get-tuple-element.92), channel_id=1, source_target_pairs={{1,0},{2,1},{3,2},{4,3},{5,4},{6,5},{7,6},{8,7},{9,8},{10,9},{11,1... | collective-permute-start | bytes 3272 | tf_op jit(solution)/shard_map/ppermute | solution.py:22
  197.1 13.7 %collective-permute-start.10 = (f32[4,64,2]{2,1,0:T(8,128)S(1)}, f32[4,64,2]{2,1,0:T(8,128)S(1)}, u32[]{:S(2)}, u32[]{:S(2)}) collective-permute-start(f32[4,64,2]{2,1,0:T(8,128)S(1)} %get-tuple-element.74), channel_id=1, source_target_pairs={{0,1},{1,2},{2,3},{3,4},{4,5},{5,6},{6,7},{7,8},{8,9},{9,10},{10,1... | collective-permute-start | bytes 6152 | tf_op jit(solution)/shard_map/ppermute | solution.py:20
  205.3 6.3 %collective-permute-start.11 = (f32[4,64,2]{2,1,0:T(8,128)S(1)}, f32[4,64,2]{2,1,0:T(8,128)S(1)}, u32[]{:S(2)}, u32[]{:S(2)}) collective-permute-start(f32[4,64,2]{2,1,0:T(8,128)S(1)} %get-tuple-element.75), channel_id=1, source_target_pairs={{1,0},{2,1},{3,2},{4,3},{5,4},{6,5},{7,6},{8,7},{9,8},{10,9},{11,1... | collective-permute-start | bytes 6152 | tf_op jit(solution)/shard_map/ppermute | solution.py:22
  207.2 4.7 %collective-permute-start.8 = (f32[4,2,128]{2,1,0:T(2,128)S(1)}, f32[4,2,128]{2,1,0:T(2,128)S(1)}, u32[]{:S(2)}, u32[]{:S(2)}) collective-permute-start(f32[4,2,128]{2,1,0:T(2,128)S(1)} %get-tuple-element.70), channel_id=1, source_target_pairs={{0,16},{16,32},{32,48},{48,64},{64,80},{80,96},{96,112},{112,128},... | collective-permute-start | bytes 12296 | tf_op jit(solution)/shard_map/ppermute | solution.py:20
  209.6 4.7 %collective-permute-start.9 = (f32[4,2,128]{2,1,0:T(2,128)S(1)}, f32[4,2,128]{2,1,0:T(2,128)S(1)}, u32[]{:S(2)}, u32[]{:S(2)}) collective-permute-start(f32[4,2,128]{2,1,0:T(2,128)S(1)} %get-tuple-element.71), channel_id=1, source_target_pairs={{16,0},{32,16},{48,32},{64,48},{80,64},{96,80},{112,96},{128,112},... | collective-permute-start | bytes 12296 | tf_op jit(solution)/shard_map/ppermute | solution.py:22
  215.0 179.7 %all-gather.11.cloned.1.call-start = ((), (), s32[]{:S(2)}) async-start(), calls=%async_computation.5 | async-start | bytes 1081344 | tf_op jit(solution)/shard_map/all_gather | solution.py:104
  215.1 4.7 %collective-permute-start.20 = (f32[2,2,128]{2,1,0:T(2,128)S(1)}, f32[2,2,128]{2,1,0:T(2,128)S(1)}, u32[]{:S(2)}, u32[]{:S(2)}) collective-permute-start(f32[2,2,128]{2,1,0:T(2,128)S(1)} %get-tuple-element.99), channel_id=1, source_target_pairs={{0,16},{16,32},{32,48},{48,64},{64,80},{80,96},{96,112},{112,128},... | collective-permute-start | bytes 6152 | tf_op jit(solution)/shard_map/ppermute | solution.py:20
  218.5 4.4 %collective-permute-start.21 = (f32[2,2,128]{2,1,0:T(2,128)S(1)}, f32[2,2,128]{2,1,0:T(2,128)S(1)}, u32[]{:S(2)}, u32[]{:S(2)}) collective-permute-start(f32[2,2,128]{2,1,0:T(2,128)S(1)} %get-tuple-element.100), channel_id=1, source_target_pairs={{16,0},{32,16},{48,32},{64,48},{80,64},{96,80},{112,96},{128,112},... | collective-permute-start | bytes 6152 | tf_op jit(solution)/shard_map/ppermute | solution.py:22
  223.0 8.3 %collective-permute-start.22 = (f32[2,68,2]{2,1,0:T(8,128)S(1)}, f32[2,68,2]{2,1,0:T(8,128)S(1)}, u32[]{:S(2)}, u32[]{:S(2)}) collective-permute-start(f32[2,68,2]{2,1,0:T(8,128)S(1)} %get-tuple-element.89), channel_id=1, source_target_pairs={{0,1},{1,2},{2,3},{3,4},{4,5},{5,6},{6,7},{7,8},{8,9},{9,10},{10,1... | collective-permute-start | bytes 3272 | tf_op jit(solution)/shard_map/ppermute | solution.py:20
  229.4 5.7 %collective-permute-start.23 = (f32[2,68,2]{2,1,0:T(8,128)S(1)}, f32[2,68,2]{2,1,0:T(8,128)S(1)}, u32[]{:S(2)}, u32[]{:S(2)}) collective-permute-start(f32[2,68,2]{2,1,0:T(8,128)S(1)} %get-tuple-element.90), channel_id=1, source_target_pairs={{1,0},{2,1},{3,2},{4,3},{5,4},{6,5},{7,6},{8,7},{9,8},{10,9},{11,1... | collective-permute-start | bytes 3272 | tf_op jit(solution)/shard_map/ppermute | solution.py:22
  297.1 13.7 %collective-permute-start.18 = (f32[4,64,2]{2,1,0:T(8,128)S(1)}, f32[4,64,2]{2,1,0:T(8,128)S(1)}, u32[]{:S(2)}, u32[]{:S(2)}) collective-permute-start(f32[4,64,2]{2,1,0:T(8,128)S(1)} %get-tuple-element.66), channel_id=1, source_target_pairs={{0,1},{1,2},{2,3},{3,4},{4,5},{5,6},{6,7},{7,8},{8,9},{9,10},{10,1... | collective-permute-start | bytes 6152 | tf_op jit(solution)/shard_map/ppermute | solution.py:20
  305.2 6.3 %collective-permute-start.19 = (f32[4,64,2]{2,1,0:T(8,128)S(1)}, f32[4,64,2]{2,1,0:T(8,128)S(1)}, u32[]{:S(2)}, u32[]{:S(2)}) collective-permute-start(f32[4,64,2]{2,1,0:T(8,128)S(1)} %get-tuple-element.67), channel_id=1, source_target_pairs={{1,0},{2,1},{3,2},{4,3},{5,4},{6,5},{7,6},{8,7},{9,8},{10,9},{11,1... | collective-permute-start | bytes 6152 | tf_op jit(solution)/shard_map/ppermute | solution.py:22
  307.1 4.7 %collective-permute-start.16 = (f32[4,2,128]{2,1,0:T(2,128)S(1)}, f32[4,2,128]{2,1,0:T(2,128)S(1)}, u32[]{:S(2)}, u32[]{:S(2)}) collective-permute-start(f32[4,2,128]{2,1,0:T(2,128)S(1)} %get-tuple-element.62), channel_id=1, source_target_pairs={{0,16},{16,32},{32,48},{48,64},{64,80},{80,96},{96,112},{112,128},... | collective-permute-start | bytes 12296 | tf_op jit(solution)/shard_map/ppermute | solution.py:20
  309.5 4.7 %collective-permute-start.17 = (f32[4,2,128]{2,1,0:T(2,128)S(1)}, f32[4,2,128]{2,1,0:T(2,128)S(1)}, u32[]{:S(2)}, u32[]{:S(2)}) collective-permute-start(f32[4,2,128]{2,1,0:T(2,128)S(1)} %get-tuple-element.63), channel_id=1, source_target_pairs={{16,0},{32,16},{48,32},{64,48},{80,64},{96,80},{112,96},{128,112},... | collective-permute-start | bytes 12296 | tf_op jit(solution)/shard_map/ppermute | solution.py:22
  315.0 4.7 %collective-permute-start.28 = (f32[2,2,128]{2,1,0:T(2,128)S(1)}, f32[2,2,128]{2,1,0:T(2,128)S(1)}, u32[]{:S(2)}, u32[]{:S(2)}) collective-permute-start(f32[2,2,128]{2,1,0:T(2,128)S(1)} %get-tuple-element.97), channel_id=1, source_target_pairs={{0,16},{16,32},{32,48},{48,64},{64,80},{80,96},{96,112},{112,128},... | collective-permute-start | bytes 6152 | tf_op jit(solution)/shard_map/ppermute | solution.py:20
  318.3 4.5 %collective-permute-start.29 = (f32[2,2,128]{2,1,0:T(2,128)S(1)}, f32[2,2,128]{2,1,0:T(2,128)S(1)}, u32[]{:S(2)}, u32[]{:S(2)}) collective-permute-start(f32[2,2,128]{2,1,0:T(2,128)S(1)} %get-tuple-element.98), channel_id=1, source_target_pairs={{16,0},{32,16},{48,32},{64,48},{80,64},{96,80},{112,96},{128,112},... | collective-permute-start | bytes 6152 | tf_op jit(solution)/shard_map/ppermute | solution.py:22
  322.9 18.1 %collective-permute-start.30 = (f32[2,68,2]{2,1,0:T(8,128)S(1)}, f32[2,68,2]{2,1,0:T(8,128)S(1)}, u32[]{:S(2)}, u32[]{:S(2)}) collective-permute-start(f32[2,68,2]{2,1,0:T(8,128)S(1)} %get-tuple-element.87), channel_id=1, source_target_pairs={{0,1},{1,2},{2,3},{3,4},{4,5},{5,6},{6,7},{7,8},{8,9},{9,10},{10,1... | collective-permute-start | bytes 3272 | tf_op jit(solution)/shard_map/ppermute | solution.py:20
  329.3 11.8 %collective-permute-start.31 = (f32[2,68,2]{2,1,0:T(8,128)S(1)}, f32[2,68,2]{2,1,0:T(8,128)S(1)}, u32[]{:S(2)}, u32[]{:S(2)}) collective-permute-start(f32[2,68,2]{2,1,0:T(8,128)S(1)} %get-tuple-element.88), channel_id=1, source_target_pairs={{1,0},{2,1},{3,2},{4,3},{5,4},{6,5},{7,6},{8,7},{9,8},{10,9},{11,1... | collective-permute-start | bytes 3272 | tf_op jit(solution)/shard_map/ppermute | solution.py:22
  331.2 17.2 %all-to-all-start.2 = ((f32[4,16,16]{2,0,1:T(4,128)}), f32[4,16,16]{2,0,1:T(4,128)S(1)}, u32[]{:S(2)}, u32[]{:S(2)}) async-start(f32[4,16,16]{2,0,1:T(4,128)} %get-tuple-element.95), calls=%async_computation.2 | async-start | bytes 65536 | tf_op jit(solution)/shard_map/all_to_all | solution.py:85
  396.9 13.7 %collective-permute-start.26 = (f32[4,64,2]{2,1,0:T(8,128)S(1)}, f32[4,64,2]{2,1,0:T(8,128)S(1)}, u32[]{:S(2)}, u32[]{:S(2)}) collective-permute-start(f32[4,64,2]{2,1,0:T(8,128)S(1)} %get-tuple-element.58), channel_id=1, source_target_pairs={{0,1},{1,2},{2,3},{3,4},{4,5},{5,6},{6,7},{7,8},{8,9},{9,10},{10,1... | collective-permute-start | bytes 6152 | tf_op jit(solution)/shard_map/ppermute | solution.py:20
  405.0 6.3 %collective-permute-start.27 = (f32[4,64,2]{2,1,0:T(8,128)S(1)}, f32[4,64,2]{2,1,0:T(8,128)S(1)}, u32[]{:S(2)}, u32[]{:S(2)}) collective-permute-start(f32[4,64,2]{2,1,0:T(8,128)S(1)} %get-tuple-element.59), channel_id=1, source_target_pairs={{1,0},{2,1},{3,2},{4,3},{5,4},{6,5},{7,6},{8,7},{9,8},{10,9},{11,1... | collective-permute-start | bytes 6152 | tf_op jit(solution)/shard_map/ppermute | solution.py:22
  407.0 4.7 %collective-permute-start.24 = (f32[4,2,128]{2,1,0:T(2,128)S(1)}, f32[4,2,128]{2,1,0:T(2,128)S(1)}, u32[]{:S(2)}, u32[]{:S(2)}) collective-permute-start(f32[4,2,128]{2,1,0:T(2,128)S(1)} %get-tuple-element.54), channel_id=1, source_target_pairs={{0,16},{16,32},{32,48},{48,64},{64,80},{80,96},{96,112},{112,128},... | collective-permute-start | bytes 12296 | tf_op jit(solution)/shard_map/ppermute | solution.py:20
  409.4 4.7 %collective-permute-start.25 = (f32[4,2,128]{2,1,0:T(2,128)S(1)}, f32[4,2,128]{2,1,0:T(2,128)S(1)}, u32[]{:S(2)}, u32[]{:S(2)}) collective-permute-start(f32[4,2,128]{2,1,0:T(2,128)S(1)} %get-tuple-element.55), channel_id=1, source_target_pairs={{16,0},{32,16},{48,32},{64,48},{80,64},{96,80},{112,96},{128,112},... | collective-permute-start | bytes 12296 | tf_op jit(solution)/shard_map/ppermute | solution.py:22
Sparse Core Ops, SparseCore 0:
  11.8 83.4 all-gather.12
  115.3 79.7 all-gather.6
  215.1 79.7 all-gather.8
  315.1 79.6 all-gather.10
where the time goes:
time: 427 us; the launch traced here: 424 us
  waiting for transfers between devices  163 us (38%)
  starting transfers between devices  127 us (30%)
  blocking collectives  70.8 us (17%)
  other arithmetic  19.7 us (5%)
  local copies, waits for them, and re-layouts  16.1 us (4%)
  between operations  14.6 us (3%)
  matrix products  12.7 us (3%)
    all_gather x4, waiting for transfers between devices, per_device(): gathered = lax.all_gather(back_east, 'gx', axis=0, tiled=True)  125 us
    ppermute x16, starting transfers between devices, with_halo(): lax.ppermute(tail, axis, [(i, (i + 1) % count) for i in range(ends)])  77 us
    all_gather x4, blocking collectives, per_device(): lax.all_gather(back_north, 'gy', axis=1, tiled=True)  70.8 us
    ppermute x16, waiting for transfers between devices, with_halo(): lax.ppermute(head, axis, [((i + 1) % count, i) for i in range(ends)])  30 us
    ppermute x16, starting transfers between devices, with_halo(): lax.ppermute(head, axis, [((i + 1) % count, i) for i in range(ends)])  25.7 us
    all_to_all x1, starting transfers between devices, per_device(): lax.all_to_all(places.reshape(1, owners_count, capacity), 'gy', split_axi...  10.1 us
    all_to_all x1, starting transfers between devices, per_device(): lax.all_to_all(misfit.reshape(steps_count, owners_count, capacity), 'gy',...  9.83 us
  transfers between devices with their start and end apart: 39, of which 18 were waited for; matrix products, arithmetic and copies ran while one was open for 8% of the time, Pallas kernels for 0%

commit v1 on v0

v1 whole, which is shorter than its diff:
```python
import functools

import jax
import jax.numpy as jnp
from jax import lax
from jax.experimental import pallas as pl
from jax.experimental.pallas import tpu as pltpu
from jax.sharding import PartitionSpec as P

mass_rate = 0.25
slope_rate = 0.3
advect_rate = 0.2
MESH = pl.DeviceIdType.MESH
f32 = jnp.float32
bf16 = jnp.bfloat16

NX_CHIPS, NZ_CHIPS, NY_CHIPS = 4, 8, 8
NGX, NGY = 32, 16
STEPS, ROWS, COLS = 4, 64, 128
XS = (1, -1, 2)
RING = (1, -1, 2, -2, 3, -3, 4)


def wrap(value, count):
    return lax.rem(value + count, count)


def split2(value):
    high = value.astype(bf16)
    low = (value - high.astype(f32)).astype(bf16)
    return high, low


def split3(value):
    first = value.astype(bf16)
    rest = value - first.astype(f32)
    second = rest.astype(bf16)
    third = (rest - second.astype(f32)).astype(bf16)
    return first, second, third


def dot(a, b):
    return lax.dot_general(a, b, (((1,), (0,)), ((), ())), preferred_element_type=f32)


def dot_nt(a, b):
    return lax.dot_general(a, b, (((1,), (1,)), ((), ())), preferred_element_type=f32)


def iota(shape, dim):
    return lax.broadcasted_iota(jnp.int32, shape, dim)


def slope_x(field, rim):
    padded = jnp.concatenate([rim, field, rim], axis=0)
    count = padded.shape[0]

    def window(shift):
        return pltpu.roll(padded, shift, 0)[8 : 8 + ROWS]

    return (window(2) - window(count - 2) + 8.0 * (window(count - 1) - window(1))) * (1.0 / 12.0)


def slope_y(field, rim):
    lane = iota(field.shape, 1)
    outer = pltpu.roll(jnp.where(lane >= COLS - 2, rim, field), 2, 1) - pltpu.roll(
        jnp.where(lane < 2, rim, field), COLS - 2, 1
    )
    inner = pltpu.roll(jnp.where(lane < 1, rim, field), COLS - 1, 1) - pltpu.roll(
        jnp.where(lane >= COLS - 1, rim, field), 1, 1
    )
    return (outer + 8.0 * inner) * (1.0 / 12.0)


def kernel(
    traj_in,
    depth_in,
    cot_in,
    line_in,
    column_in,
    owner_in,
    cell_in,
    obs_in,
    weight_in,
    state_out,
    depth_out,
    residual_out,
    traj,
    depth,
    line,
    column,
    owner,
    cell,
    obs,
    weight,
    surf,
    ebuf,
    nbuf,
    eedge,
    nedge,
    xh_out,
    xh_in,
    yh_out,
    yh_in,
    lrim,
    crim,
    tx_in,
    ty_out,
    ty_in,
    gout,
    gin,
    rout,
    rin,
    onehot,
    ll,
    ct,
    cx,
    nn,
    ae,
    fields3,
    forcing,
    acc,
    base,
    coef,
    load_sem,
    e_send,
    e_zrecv,
    e_xrecv,
    n_send,
    n_yrecv,
    n_crecv,
    ee_send,
    ee_recv,
    ne_send,
    ne_recv,
    xh_send,
    xh_recv,
    yh_send,
    yh_recv,
    once_send,
    once_recv,
):
    gx = lax.axis_index("gx")
    gy = lax.axis_index("gy")
    x, z = lax.div(gx, NZ_CHIPS), lax.rem(gx, NZ_CHIPS)
    y, core = lax.div(gy, 2), lax.rem(gy, 2)
    nslot = core * NY_CHIPS + y

    def at_x(d):
        return (wrap(x + d, NX_CHIPS) * NZ_CHIPS + z, gy)

    def at_z(d):
        return (x * NZ_CHIPS + wrap(z + d, NZ_CHIPS), gy)

    def at_y(d):
        return (gx, wrap(y + d, NY_CHIPS) * 2 + core)

    sibling = (gx, y * 2 + 1 - core)
    above, below = (wrap(gx - 1, NGX), gy), (wrap(gx + 1, NGX), gy)
    before, after = (gx, wrap(gy - 1, NGY)), (gx, wrap(gy + 1, NGY))

    has_above = jnp.where(gx > 0, 1.0, 0.0).astype(f32)
    has_below = jnp.where(gx < NGX - 1, 1.0, 0.0).astype(f32)
    has_before = jnp.where(gy > 0, 1.0, 0.0).astype(f32)
    has_after = jnp.where(gy < NGY - 1, 1.0, 0.0).astype(f32)

    def merge_x(top, bottom):
        return jnp.where(iota(top.shape, 0) >= 4, top * has_above, bottom * has_below)

    def merge_y(left, right):
        return jnp.where(iota(left.shape, 0) >= 4, left * has_before, right * has_after)

    def send(src, dst, send_sem, recv_sem, device):
        pltpu.make_async_remote_copy(
            src_ref=src,
            dst_ref=dst,
            send_sem=send_sem,
            recv_sem=recv_sem,
            device_id=device,
            device_id_type=MESH,
        ).start()

    def arrive(ref, sem):
        pltpu.make_async_copy(ref, ref, sem).wait()

    loads = [
        pltpu.make_async_copy(src, dst, load_sem.at[i])
        for i, (src, dst) in enumerate(
            [
                (cot_in.at[0], surf),
                (cot_in.at[1], ebuf.at[0, gx]),
                (cot_in.at[2], nbuf.at[0, nslot]),
                (traj_in, traj),
                (depth_in, depth),
                (line_in, line),
                (column_in, column),
                (owner_in, owner),
                (cell_in, cell),
                (obs_in, obs),
                (weight_in, weight),
            ]
        )
    ]
    for copy in loads:
        copy.start()

    barrier = pltpu.get_barrier_semaphore()
    peers = (
        [at_x(d) for d in XS]
        + [at_z(d) for d in RING]
        + [(gx, lax.rem(gy + d, NGY)) for d in range(1, NGY)]
        + [above, below]
    )
    for peer in peers:
        pl.semaphore_signal(barrier, inc=1, device_id=peer, device_id_type=MESH)
    for copy in loads:
        copy.wait()
    pl.semaphore_wait(barrier, len(peers))

    def start_step(s):
        mine = ebuf.at[s, gx]
        for i, d in enumerate(RING):
            send(mine, mine, e_send, e_zrecv.at[s, i], at_z(d))
        own = nbuf.at[s, nslot]
        for i, d in enumerate(RING):
            send(own, own, n_send, n_yrecv.at[s, i], at_y(d))
        for j, d in enumerate(XS):
            send(mine, mine, e_send, e_xrecv.at[s, j], at_x(d))
        surface = surf[...]
        east = mine[...]
        north = own[...]
        xh_out[s, 0, 0] = surface[0:8]
        xh_out[s, 0, 1] = north[0:8]
        xh_out[s, 1, 0] = surface[ROWS - 8 :]
        xh_out[s, 1, 1] = north[ROWS - 8 :]
        send(xh_out.at[s, 0], xh_in.at[s, 1], xh_send, xh_recv.at[s, 1], above)
        send(xh_out.at[s, 1], xh_in.at[s, 0], xh_send, xh_recv.at[s, 0], below)
        turned = jnp.concatenate([surface, east], axis=0).T
        yh_out[s, 0] = turned[0:8]
        yh_out[s, 1] = turned[COLS - 8 :]
        send(yh_out.at[s, 0], yh_in.at[s, 1], yh_send, yh_recv.at[s, 1], before)
        send(yh_out.at[s, 1], yh_in.at[s, 0], yh_send, yh_recv.at[s, 0], after)
        send(own, own, n_send, n_crecv.at[s], sibling)

    def start_once():
        both = pl.ds(1, 2)
        send(traj.at[:, both, pl.ds(0, 8)], tx_in.at[1], once_send.at[0], once_recv.at[0], above)
        send(
            traj.at[:, both, pl.ds(ROWS - 8, 8)],
            tx_in.at[0],
            once_send.at[0],
            once_recv.at[1],
            below,
        )
        for t in range(STEPS):
            turned = jnp.concatenate([traj[t, 1], traj[t, 2]], axis=0).T
            ty_out[0, t] = turned[0:8]
            ty_out[1, t] = turned[COLS - 8 :]
        send(ty_out.at[0], ty_in.at[1], once_send.at[1], once_recv.at[2], before)
        send(ty_out.at[1], ty_in.at[0], once_send.at[1], once_recv.at[3], after)
        owners = owner[...]
        lane = iota((NGY, COLS), 1)
        member = jnp.where(iota((NGY, COLS), 0) == owners, 1.0, 0.0).astype(f32)
        upper = jnp.where(iota((COLS, COLS), 0) <= iota((COLS, COLS), 1), 1.0, 0.0).astype(bf16)
        counted = dot(member.astype(bf16), upper)
        rank = jnp.sum(counted * member, axis=0, keepdims=True).astype(jnp.int32) - 1
        target = owners * 16 + rank
        picked = jnp.where(iota((2 * COLS, COLS), 0) == target, 1.0, 0.0).astype(bf16)
        onehot[...] = picked
        cells = cell[...]
        row = lax.shift_right_logical(cells, 7).astype(f32)
        col = lax.bitwise_and(cells, COLS - 1).astype(f32)
        payload = jnp.concatenate([obs[...], weight[...], row, col, jnp.ones_like(row)], axis=0)
        placed = dot_nt(jnp.concatenate([p.astype(f32) for p in split3(payload)], axis=0).astype(bf16), picked)
        placed = placed[0:8] + placed[8:16] + placed[16:24]
        del lane
        mod = lax.rem(gy, 8)
        for d in range(NGY):
            half = placed[:, (d // 8) * COLS : (d // 8 + 1) * COLS]
            gout[d] = pltpu.roll(half, wrap(mod - d % 8, 8) * 16, 1)
        gin[gy] = gout[gy]
        for d in range(1, NGY):
            peer = lax.rem(gy + d, NGY)
            send(gout.at[peer], gin.at[gy], once_send.at[2], once_recv.at[4], (gx, peer))
        send(line.at[pl.ds(0, 8)], lrim.at[1], once_send.at[3], once_recv.at[5], above)
        send(line.at[pl.ds(ROWS - 8, 8)], lrim.at[0], once_send.at[3], once_recv.at[6], below)
        send(column.at[pl.ds(0, 8)], crim.at[1], once_send.at[4], once_recv.at[7], before)
        send(column.at[pl.ds(COLS - 8, 8)], crim.at[0], once_send.at[4], once_recv.at[8], after)

    def gauges():
        arrive(gin.at[pl.ds(0, NGY - 1)], once_recv.at[4])
        for t in range(STEPS):
            for p, piece in enumerate(split3(traj[t, 0])):
                fields3[pl.ds((p * STEPS + t) * ROWS, ROWS)] = piece
        mod = lax.rem(gy, 8)
        lane8 = iota((8, COLS), 1)
        total = None
        for half in range(2):
            record = gin[half * 8]
            for k in range(1, 8):
                record = jnp.where(lax.shift_right_logical(lane8, 4) == k, gin[half * 8 + k], record)
            valid = record[7:8] > 0.5
            row = record[5:6].astype(jnp.int32)
            col = record[6:7].astype(jnp.int32)
            in_col = jnp.where((iota((COLS, COLS), 0) == col) & valid, 1.0, 0.0).astype(bf16)
            in_row = jnp.where(iota((ROWS, COLS), 0) == row, 1.0, 0.0).astype(f32)
            seen = dot(fields3[...], in_col)
            misfits, parts = [], [[], [], []]
            for t in range(STEPS):
                at = [seen[(p * STEPS + t) * ROWS : (p * STEPS + t + 1) * ROWS] for p in range(3)]
                value = jnp.sum((at[0] + at[1] + at[2]) * in_row, axis=0, keepdims=True)
                misfit = jnp.where(valid, value - record[t : t + 1], 0.0)
                misfits.append(misfit)
                for p, piece in enumerate(split3(record[4:5] * misfit)):
                    parts[p].append((in_row * piece.astype(f32)).astype(bf16))
            back = jnp.concatenate(misfits + [jnp.zeros((4, COLS), f32)], axis=0)
            for k in range(8):
                rout[half * 8 + k] = pltpu.roll(back, wrap(mod - k, 8) * 16, 1)
            spread = dot_nt(jnp.concatenate(parts[0] + parts[1] + parts[2], axis=0), in_col)
            total = spread if total is None else total + spread
        size = STEPS * ROWS
        total = total[0:size] + total[size : 2 * size] + total[2 * size :]
        for t in range(STEPS):
            forcing[t] = total[t * ROWS : (t + 1) * ROWS]
        rin[gy] = rout[gy]
        for d in range(1, NGY):
            peer = lax.rem(gy + d, NGY)
            send(rout.at[peer], rin.at[gy], once_send.at[5], once_recv.at[9], (gx, peer))

    def prepare():
        arrive(lrim.at[0], once_recv.at[5])
        arrive(lrim.at[0], once_recv.at[6])
        arrive(crim.at[0], once_recv.at[7])
        arrive(crim.at[0], once_recv.at[8])
        high, low = split2(line[...])
        ll[pl.ds(0, ROWS)] = high
        ll[pl.ds(ROWS, ROWS)] = low
        rim = merge_x(lrim[0], lrim[1])
        high = rim.astype(bf16).astype(f32)
        ll[pl.ds(2 * ROWS, 16)] = jnp.concatenate([high, rim - high], axis=0).astype(bf16)
        rim = merge_y(crim[0], crim[1])
        high = rim.astype(bf16).astype(f32)
        cx[...] = jnp.concatenate([high, rim - high], axis=0).astype(bf16)
        for k in range(NGY):
            at = slice(k * COLS, (k + 1) * COLS)
            high, low = split2(column[:, at].T)
            ct[at, 0:COLS] = high
            ct[at, COLS : 2 * COLS] = low

    def rim_y(left, right):
        merged = merge_y(left, right)
        return jnp.concatenate([merged, jnp.zeros((COLS - 16, COLS), f32), merged], axis=0).T

    def step(s, carry):
        t = STEPS - 1 - s
        start_step(s)

        @pl.when(s == 0)
        def _():
            start_once()

        def from_z(i, d):
            block = ebuf.at[s, x * NZ_CHIPS + wrap(z - d, NZ_CHIPS)]
            arrive(block, e_zrecv.at[s, i])
            for j, a in enumerate(XS):
                send(block, block, e_send, e_xrecv.at[s, j], at_x(a))

        def from_y(i, d):
            block = nbuf.at[s, core * NY_CHIPS + wrap(y - d, NY_CHIPS)]
            arrive(block, n_yrecv.at[s, i])
            send(block, block, n_send, n_crecv.at[s], sibling)

        from_z(0, RING[0])
        from_z(1, RING[1])
        arrive(xh_in.at[s, 0], xh_recv.at[s, 0])
        arrive(xh_in.at[s, 1], xh_recv.at[s, 1])
        nedge[s, nslot] = merge_x(xh_in[s, 0, 1], xh_in[s, 1, 1])
        for d in RING:
            send(nedge.at[s, nslot], nedge.at[s, nslot], ne_send, ne_recv.at[s, 0], at_y(d))
        arrive(yh_in.at[s, 0], yh_recv.at[s, 0])
        arrive(yh_in.at[s, 0], yh_recv.at[s, 1])
        eedge[s, gx] = merge_y(yh_in[s, 0], yh_in[s, 1])
        for d in RING:
            send(eedge.at[s, gx], eedge.at[s, gx], ee_send, ee_recv.at[s, 0], at_z(d))
        from_y(0, RING[0])
        from_y(1, RING[1])
        from_z(2, RING[2])
        from_z(3, RING[3])

        @pl.when(s == 0)
        def _():
            arrive(tx_in.at[0], once_recv.at[0])
            arrive(tx_in.at[0], once_recv.at[1])
            arrive(ty_in.at[0], once_recv.at[2])
            arrive(ty_in.at[0], once_recv.at[3])

        surface = surf[...]
        east, north = traj[t, 1], traj[t, 2]
        whole = depth[...] + traj[t, 0]
        rim_surface = rim_y(yh_in[s, 0], yh_in[s, 1])[0:ROWS]
        flux_x = mass_rate * slope_x(surface, merge_x(xh_in[s, 0, 0], xh_in[s, 1, 0]))
        flux_y = mass_rate * slope_y(surface, rim_surface)
        gain = east * flux_x + north * flux_y
        depth_out[...] = jnp.where(s == 0, 0.0, depth_out[...]) + gain
        base[0] = surface + gain
        base[1] = whole * flux_x
        base[2] = whole * flux_y
        from_y(2, RING[2])
        from_y(3, RING[3])
        from_z(4, RING[4])
        from_z(5, RING[5])
        rims = rim_y(ty_in[0, t], ty_in[1, t])
        east_x = merge_x(tx_in[0, t, 0], tx_in[1, t, 0])
        north_x = merge_x(tx_in[0, t, 1], tx_in[1, t, 1])
        north_y = rims[ROWS:]
        coef[0] = 1.0 - advect_rate * slope_x(east, east_x)
        coef[1] = advect_rate * slope_x(north, north_x)
        coef[2] = advect_rate * slope_y(east, rims[0:ROWS])
        coef[3] = 1.0 - advect_rate * slope_y(north, north_y)
        from_z(6, RING[6])
        arrive(eedge.at[s, pl.ds(0, NZ_CHIPS - 1)], ee_recv.at[s, 0])
        line_edges = eedge.at[s, pl.ds(x * NZ_CHIPS, NZ_CHIPS)]
        for a in XS:
            send(line_edges, line_edges, ee_send, ee_recv.at[s, 1], at_x(a))
        from_y(4, RING[4])
        from_y(5, RING[5])
        from_y(6, RING[6])
        arrive(nedge.at[s, pl.ds(0, NY_CHIPS - 1)], ne_recv.at[s, 0])
        column_edges = nedge.at[s, pl.ds(core * NY_CHIPS, NY_CHIPS)]
        send(column_edges, column_edges, ne_send, ne_recv.at[s, 1], sibling)

        @pl.when(s == 0)
        def _():
            prepare()
            gauges()

        arrive(nbuf.at[s, pl.ds(0, NY_CHIPS)], n_crecv.at[s])
        arrive(nedge.at[s, pl.ds(0, NY_CHIPS)], ne_recv.at[s, 1])
        for k in range(NGY):
            at = ((k % NY_CHIPS) * 2 + k // NY_CHIPS) * COLS
            at = slice(at, at + COLS)
            high, low = split2(nbuf[s, k])
            nn[0:ROWS, at] = high
            nn[ROWS : 2 * ROWS, at] = low
            rim = nedge[s, k]
            high = rim.astype(bf16).astype(f32)
            nn[2 * ROWS : 2 * ROWS + 16, at] = jnp.concatenate([high, rim - high], axis=0).astype(bf16)
        product = dot(nn[...], ct[...])

        def joined(product):
            left, right = product[:, 0:COLS], product[:, COLS:]
            inner = left[0:ROWS] + (right[0:ROWS] + left[ROWS : 2 * ROWS])
            at = 2 * ROWS
            rim = left[at : at + 8] + (right[at : at + 8] + left[at + 8 : at + 16])
            return inner, rim

        def sides(product):
            rim = product[0:ROWS] + (pltpu.roll(product[0:ROWS], COLS - 8, 1) + product[ROWS : 2 * ROWS])
            return jnp.where(iota((ROWS, COLS), 1) < 8, rim, pltpu.roll(rim, COLS - 8, 1))

        def widened(product):
            return jnp.concatenate([product, jnp.zeros((2 * ROWS, COLS - 16), f32)], axis=1)

        column_adjoint, column_x = joined(product)
        column_y = sides(widened(dot_nt(nn[0 : 2 * ROWS, :], cx[...])))

        def line_part(at):
            blocks = ebuf[s, pl.ds(at * NZ_CHIPS, NZ_CHIPS)].reshape(NZ_CHIPS * ROWS, COLS)
            high, low = split2(blocks)
            lanes = pl.ds(pl.multiple_of(at * (NZ_CHIPS * ROWS), NZ_CHIPS * ROWS), NZ_CHIPS * ROWS)
            return dot(ll[:, lanes], jnp.concatenate([high, low], axis=1))

        acc[...] = line_part(x)
        for j in range(2):
            at = wrap(x - XS[j], NX_CHIPS)
            arrive(ebuf.at[s, pl.ds(0, NZ_CHIPS)], e_xrecv.at[s, j])
            acc[...] += line_part(at)
        arrive(eedge.at[s, pl.ds(0, 3 * NZ_CHIPS)], ee_recv.at[s, 1])
        lane = iota((8, COLS), 1)
        for k in range(NGX // 2):
            rim = jnp.where(lane < ROWS, pltpu.roll(eedge[s, 2 * k], ROWS, 1), eedge[s, 2 * k + 1])
            high = rim.astype(bf16).astype(f32)
            ae[:, k * COLS : (k + 1) * COLS] = jnp.concatenate([high, rim - high], axis=0).astype(bf16)
        line_y = sides(widened(dot_nt(ll[0 : 2 * ROWS, :], ae[...])))
        arrive(ebuf.at[s, pl.ds(0, NZ_CHIPS)], e_xrecv.at[s, 2])
        line_adjoint, line_x = joined(acc[...] + line_part(wrap(x - XS[2], NX_CHIPS)))

        along_x = slope_x(line_adjoint, line_x)
        along_y = slope_y(column_adjoint, column_y)
        surf[...] = base[0] + forcing[t] + slope_rate * (along_x + along_y)
        mixed = slope_x(east * line_adjoint, east_x * line_x) + slope_y(
            north * line_adjoint, north_y * line_y
        )
        ebuf[s + 1, gx] = (
            line_adjoint * coef[0] - column_adjoint * coef[1] + advect_rate * mixed + base[1]
        )
        mixed = slope_x(east * column_adjoint, east_x * column_x) + slope_y(
            north * column_adjoint, north_y * column_y
        )
        nbuf[s + 1, nslot] = (
            column_adjoint * coef[3] - line_adjoint * coef[2] + advect_rate * mixed + base[2]
        )

        arrive(ebuf.at[s, pl.ds(0, NGX - 1)], e_send)
        arrive(nbuf.at[s, pl.ds(0, NGY - 1)], n_send)
        arrive(eedge.at[s, pl.ds(0, NGX - 1)], ee_send)
        arrive(nedge.at[s, pl.ds(0, NGY - 1)], ne_send)
        arrive(xh_out.at[s], xh_send)
        arrive(yh_out.at[s], yh_send)
        return carry

    lax.fori_loop(0, STEPS, step, 0)

    state_out[0] = surf[...]
    state_out[1] = ebuf[STEPS, gx]
    state_out[2] = nbuf[STEPS, nslot]

    arrive(rin.at[pl.ds(0, NGY - 1)], once_recv.at[9])
    lane8 = iota((8, COLS), 1)
    halves = []
    for half in range(2):
        record = rin[half * 8]
        for k in range(1, 8):
            record = jnp.where(lax.shift_right_logical(lane8, 4) == k, rin[half * 8 + k], record)
        halves.append(record)
    returned = jnp.concatenate(halves, axis=1)
    pieces = jnp.concatenate([p.astype(f32) for p in split3(returned)], axis=0).astype(bf16)
    found = dot(pieces, onehot[...])
    residual_out[...] = found[0:4] + found[8:12] + found[16:20]
    arrive(tx_in, once_send.at[0])
    arrive(ty_out, once_send.at[1])
    arrive(gout.at[pl.ds(0, NGY - 1)], once_send.at[2])
    arrive(lrim, once_send.at[3])
    arrive(crim, once_send.at[4])
    arrive(rout.at[pl.ds(0, NGY - 1)], once_send.at[5])


def per_device(
    trajectory,
    depth,
    cotangent,
    line_inverse,
    column_inverse,
    gauge_owner,
    gauge_cell,
    gauge_obs,
    gauge_weight,
):
    vmem = pltpu.VMEM
    dma = pltpu.SemaphoreType.DMA
    scratch = [
        vmem((STEPS, 3, ROWS, COLS), f32),
        vmem((ROWS, COLS), f32),
        vmem((ROWS, 2048), f32),
        vmem((COLS, 2048), f32),
        vmem((1, COLS), jnp.int32),
        vmem((1, COLS), jnp.int32),
        vmem((STEPS, COLS), f32),
        vmem((1, COLS), f32),
        vmem((ROWS, COLS), f32),
        vmem((STEPS + 1, NGX, ROWS, COLS), f32),
        vmem((STEPS + 1, NGY, ROWS, COLS), f32),
        vmem((STEPS, NGX, 8, COLS), f32),
        vmem((STEPS, NGY, 8, COLS), f32),
        vmem((STEPS, 2, 2, 8, COLS), f32),
        vmem((STEPS, 2, 2, 8, COLS), f32),
        vmem((STEPS, 2, 8, COLS), f32),
        vmem((STEPS, 2, 8, COLS), f32),
        vmem((2, 8, 2048), f32),
        vmem((2, 8, 2048), f32),
        vmem((2, STEPS, 2, 8, COLS), f32),
        vmem((2, STEPS, 8, COLS), f32),
        vmem((2, STEPS, 8, COLS), f32),
        vmem((NGY, 8, COLS), f32),
        vmem((NGY, 8, COLS), f32),
        vmem((NGY, 8, COLS), f32),
        vmem((NGY, 8, COLS), f32),
        vmem((2 * COLS, COLS), bf16),
        vmem((2 * ROWS + 16, 2048), bf16),
        vmem((2048, 2 * COLS), bf16),
        vmem((16, 2048), bf16),
        vmem((2 * ROWS + 16, 2048), bf16),
        vmem((16, 2048), bf16),
        vmem((3 * STEPS * ROWS, COLS), bf16),
        vmem((STEPS, ROWS, COLS), f32),
        vmem((2 * ROWS + 16, 2 * COLS), f32),
        vmem((3, ROWS, COLS), f32),
        vmem((4, ROWS, COLS), f32),
        dma((11,)),
        dma,
        dma((STEPS, 7)),
        dma((STEPS, 3)),
        dma,
        dma((STEPS, 7)),
        dma((STEPS,)),
        dma,
        dma((STEPS, 2)),
        dma,
        dma((STEPS, 2)),
        dma,
        dma((STEPS, 2)),
        dma,
        dma((STEPS, 2)),
        dma((6,)),
        dma((10,)),
    ]
    anywhere = pl.BlockSpec(memory_space=pl.ANY)
    here = pl.BlockSpec(memory_space=pltpu.VMEM)
    return pl.pallas_call(
        kernel,
        name="adjoint",
        out_shape=(
            jax.ShapeDtypeStruct((3, ROWS, COLS), f32),
            jax.ShapeDtypeStruct((ROWS, COLS), f32),
            jax.ShapeDtypeStruct((STEPS, COLS), f32),
        ),
        in_specs=[anywhere] * 9,
        out_specs=(here, here, here),
        scratch_shapes=scratch,
        compiler_params=pltpu.CompilerParams(
            collective_id=0, has_side_effects=True, vmem_limit_bytes=48 * 2**20
        ),
    )(
        trajectory,
        depth,
        cotangent,
        line_inverse,
        column_inverse,
        gauge_owner.reshape(1, COLS),
        gauge_cell.reshape(1, COLS),
        gauge_obs,
        gauge_weight.reshape(1, COLS),
    )


def solution(mesh):
    return jax.shard_map(
        per_device,
        mesh=mesh,
        in_specs=(
            P(None, None, "gx", "gy"),
            P("gx", "gy"),
            P(None, "gx", "gy"),
            P("gx", None),
            P("gy", None),
            P(("gx", "gy"), None),
            P(("gx", "gy")),
            P(None, ("gx", "gy")),
            P(("gx", "gy")),
        ),
        out_specs=(P(None, "gx", "gy"), P("gx", "gy"), P(None, ("gx", "gy"))),
        check_vma=False,
    )
```

time: 427 us -> 102 us (0.24)
  waiting for transfers between devices: 163 us -> 0 us
  starting transfers between devices: 127 us -> 0 us
  Pallas kernels: 0 us -> 92.7 us
  blocking collectives: 70.8 us -> 0 us
  other arithmetic: 19.7 us -> 0 us
  between operations: 14.6 us -> 0.68 us
  matrix products: 12.7 us -> 0 us
  local copies, waits for them, and re-layouts: 16.1 us -> 7.42 us
    all_gather x4 -> x0, waiting for transfers between devices: 125 us -> none  [per_device(): gathered = lax.all_gather(back_east, 'gx', axis=0, tiled=True)]
    ppermute x32 -> x0, starting transfers between devices: 103 us -> none  [the longest x16 77 us: with_halo(): lax.ppermute(tail, axis, [(i, (i + 1) % count) for i in range(ends)])]
    pallas_call x0 -> x1, Pallas kernels: none -> 92.7 us  [per_device(): pl.pallas_call(kernel, name='adjoint', out_shape=(jax.ShapeDtypeStruct((3...]
    all_gather x4 -> x0, blocking collectives: 70.8 us -> none  [per_device(): lax.all_gather(back_north, 'gy', axis=1, tiled=True)]
    ppermute x32 -> x0, waiting for transfers between devices: 30 us -> none  [the longest x16 30 us: with_halo(): lax.ppermute(head, axis, [((i + 1) % count, i) for i in range(ends)])]
    all_to_all x3 -> x0, starting transfers between devices: 24.6 us -> none  [the longest x1 10.1 us: per_device(): lax.all_to_all(places.reshape(1, owners_count, capacity), 'gy', split_axi...]
    dot_general x8 -> x0, matrix products: 12.7 us -> none  [the longest x4 7.95 us: per_device(): line_adjoint = jnp.dot(line_inverse, gathered, precision=highest)]
    scatter-add x4 -> x0, other arithmetic: 8.35 us -> none  [per_device(): new_surface.reshape(rows * cols).at[cell_list].add(forcing[section])]
  transfers between devices with their start and end apart: 39 -> 0, of which waited for: 18 -> 0; matrix products, arithmetic and copies ran while one was open for 8% -> 0% of each run, Pallas kernels for 0% -> 0%
where the time goes in v1:
time: 102 us; the launch traced here: 101 us
  Pallas kernels  92.7 us (91%)
  local copies, waits for them, and re-layouts  7.42 us (7%)
    pallas_call x1, Pallas kernels, per_device(): pl.pallas_call(kernel, name='adjoint', out_shape=(jax.ShapeDtypeStruct((3...  92.7 us
    unnamed x21, local copies, waits for them, and re-layouts  7.42 us

profile of v1, /device:TPU:1, one launch (start us, length us, event | category | flops | bytes accessed | tf_op | source)
XLA Modules:
  0.0 100.8 jit_solution(13638801310090726499)
XLA Ops:
  0.6 0.0 copy-start.5
  0.6 0.0 copy-start.6
  0.7 0.0 copy-start.7
  0.7 0.0 copy-start.8
  0.7 0.6 copy-done.5
  1.3 0.0 copy-done.6
  1.3 0.0 copy-done.7
  1.3 0.0 copy-done.8
  1.3 0.0 copy-start
  1.3 1.2 %copy-done = f32[128,2048]{1,0:T(8,128)S(1)} copy-done((f32[128,2048]{1,0:T(8,128)S(1)}, f32[128,2048]{1,0:T(8,128)}, u32[]{:S(2)}) %copy-start) | copy-done | bytes 1048600
  2.6 0.0 copy-start.1
  2.6 1.0 %copy-done.1 = f32[64,2048]{1,0:T(8,128)S(1)} copy-done((f32[64,2048]{1,0:T(8,128)S(1)}, f32[64,2048]{1,0:T(8,128)}, u32[]{:S(2)}) %copy-start.1) | copy-done | bytes 524312
  3.6 0.0 copy-start.2
  3.6 1.0 copy-done.2
  4.6 0.0 copy-start.3
  4.6 0.9 copy-done.3
  5.5 0.0 copy-start.4
  5.5 0.8 copy-done.4
  6.3 92.7 %adjoint.1 = (f32[3,64,128]{2,1,0:T(8,128)S(1)}, f32[64,128]{1,0:T(8,128)S(1)}, f32[4,128]{1,0:T(4,128)S(1)}) custom-call(f32[4,3,64,128]{3,2,1,0:T(8,128)S(1)} %copy-done.2, f32[64,128]{1,0:T(8,128)S(1)} %copy-done.4, f32[3,64,128]{2,1,0:T(8,128)S(1)} %copy-done.3, f32[64,2048]{1,0:T(8,128)S(1)} %copy-done.1, f32[128,2048]{1,0:T(8,128)S(1)} %copy-done, ...), custom_call_target="tpu_custom_call" | custom-call | tf_op jit(solution)/shard_map/adjoint/pallas_call | solution.py:609
  98.9 0.6 copy.15
  99.6 0.6 copy.16
  100.2 0.6 copy.17
Async XLA Ops:
  0.6 0.7 copy-start.5
  0.6 0.7 copy-start.6
  0.7 0.7 copy-start.7
  0.7 0.7 copy-start.8
  1.3 1.2 %copy-start = (f32[128,2048]{1,0:T(8,128)S(1)}, f32[128,2048]{1,0:T(8,128)}, u32[]{:S(2)}) copy-start(f32[128,2048]{1,0:T(8,128)} %column_in.1) | copy-start | bytes 3145732
  2.6 1.0 %copy-start.1 = (f32[64,2048]{1,0:T(8,128)S(1)}, f32[64,2048]{1,0:T(8,128)}, u32[]{:S(2)}) copy-start(f32[64,2048]{1,0:T(8,128)} %line_in.1) | copy-start | bytes 1572868
  3.6 1.0 copy-start.2
  4.6 0.9 copy-start.3
  5.5 0.8 copy-start.4

commit v2 on v1

v2 whole, which is shorter than its diff:
```python
import functools

import jax
import jax.numpy as jnp
from jax import lax
from jax.experimental import pallas as pl
from jax.experimental.pallas import tpu as pltpu
from jax.sharding import PartitionSpec as P

mass_rate = 0.25
slope_rate = 0.3
advect_rate = 0.2
MESH = pl.DeviceIdType.MESH
f32 = jnp.float32
bf16 = jnp.bfloat16

NX_CHIPS, NZ_CHIPS, NY_CHIPS = 4, 8, 8
NGX, NGY = 32, 16
STEPS, ROWS, COLS = 4, 64, 128
XS = (1, -1, 2)
RING = (1, -1, 2, -2, 3, -3, 4)


def wrap(value, count):
    return lax.rem(value + count, count)


def split2(value):
    high = value.astype(bf16)
    low = (value - high.astype(f32)).astype(bf16)
    return high, low


def split3(value):
    first = value.astype(bf16)
    rest = value - first.astype(f32)
    second = rest.astype(bf16)
    third = (rest - second.astype(f32)).astype(bf16)
    return first, second, third


def dot(a, b):
    return lax.dot_general(a, b, (((1,), (0,)), ((), ())), preferred_element_type=f32)


def dot_nt(a, b):
    return lax.dot_general(a, b, (((1,), (1,)), ((), ())), preferred_element_type=f32)


def iota(shape, dim):
    return lax.broadcasted_iota(jnp.int32, shape, dim)


def slope_x(field, rim):
    padded = jnp.concatenate([rim, field, rim], axis=0)
    count = padded.shape[0]

    def window(shift):
        return pltpu.roll(padded, shift, 0)[8 : 8 + ROWS]

    return (window(2) - window(count - 2) + 8.0 * (window(count - 1) - window(1))) * (1.0 / 12.0)


def slope_y(field, rim):
    lane = iota(field.shape, 1)
    outer = pltpu.roll(jnp.where(lane >= COLS - 2, rim, field), 2, 1) - pltpu.roll(
        jnp.where(lane < 2, rim, field), COLS - 2, 1
    )
    inner = pltpu.roll(jnp.where(lane < 1, rim, field), COLS - 1, 1) - pltpu.roll(
        jnp.where(lane >= COLS - 1, rim, field), 1, 1
    )
    return (outer + 8.0 * inner) * (1.0 / 12.0)


def kernel(
    traj_in,
    depth_in,
    cot_in,
    line_in,
    column_in,
    owner_in,
    cell_in,
    obs_in,
    weight_in,
    state_out,
    depth_out,
    residual_out,
    traj,
    depth,
    line,
    column,
    owner,
    cell,
    obs,
    weight,
    surf,
    ebuf,
    nbuf,
    eedge,
    nedge,
    xh_out,
    xh_in,
    yh_out,
    yh_in,
    lrim,
    crim,
    tx_in,
    ty_out,
    ty_in,
    gout,
    gin,
    rout,
    rin,
    lpart,
    lrimpart,
    lmerged,
    pout,
    pin,
    onehot,
    ll,
    ct,
    cx,
    nn,
    ae,
    ez,
    fields3,
    forcing,
    base,
    coef,
    load_sem,
    e_send,
    e_recv,
    p_send,
    p_recv,
    n_send,
    n_yrecv,
    n_crecv,
    ee_send,
    ee_recv,
    ne_send,
    ne_recv,
    xh_send,
    xh_recv,
    yh_send,
    yh_recv,
    l_send,
    l_recv,
    once_send,
    once_recv,
):
    gx = lax.axis_index("gx")
    gy = lax.axis_index("gy")
    x, z = lax.div(gx, NZ_CHIPS), lax.rem(gx, NZ_CHIPS)
    y, core = lax.div(gy, 2), lax.rem(gy, 2)
    nslot = core * NY_CHIPS + y

    def at_x(d):
        return (wrap(x + d, NX_CHIPS) * NZ_CHIPS + z, gy)

    def at_z(d):
        return (x * NZ_CHIPS + wrap(z + d, NZ_CHIPS), gy)

    def at_y(d):
        return (gx, wrap(y + d, NY_CHIPS) * 2 + core)

    sibling = (gx, y * 2 + 1 - core)
    above, below = (wrap(gx - 1, NGX), gy), (wrap(gx + 1, NGX), gy)
    before, after = (gx, wrap(gy - 1, NGY)), (gx, wrap(gy + 1, NGY))

    has_above = jnp.where(gx > 0, 1.0, 0.0).astype(f32)
    has_below = jnp.where(gx < NGX - 1, 1.0, 0.0).astype(f32)
    has_before = jnp.where(gy > 0, 1.0, 0.0).astype(f32)
    has_after = jnp.where(gy < NGY - 1, 1.0, 0.0).astype(f32)

    def merge_x(top, bottom):
        return jnp.where(iota(top.shape, 0) >= 4, top * has_above, bottom * has_below)

    def merge_y(left, right):
        return jnp.where(iota(left.shape, 0) >= 4, left * has_before, right * has_after)

    def send(src, dst, send_sem, recv_sem, device):
        pltpu.make_async_remote_copy(
            src_ref=src,
            dst_ref=dst,
            send_sem=send_sem,
            recv_sem=recv_sem,
            device_id=device,
            device_id_type=MESH,
        ).start()

    def arrive(ref, sem):
        pltpu.make_async_copy(ref, ref, sem).wait()

    loads = [
        pltpu.make_async_copy(src, dst, load_sem.at[i])
        for i, (src, dst) in enumerate(
            [
                (cot_in.at[0], surf),
                (cot_in.at[1], ebuf.at[0, z]),
                (cot_in.at[2], nbuf.at[0, nslot]),
                (traj_in, traj),
                (depth_in, depth),
                (line_in, line),
                (column_in, column),
                (owner_in, owner),
                (cell_in, cell),
                (obs_in, obs),
                (weight_in, weight),
            ]
        )
    ]
    for copy in loads:
        copy.start()

    barrier = pltpu.get_barrier_semaphore()
    peers = (
        [at_z(d) for d in reversed(RING)]
        + [(gx, lax.rem(gy + d, NGY)) for d in (8, 9, 7, 10, 6, 11, 5, 12, 4, 13, 3, 14, 2, 15, 1)]
        + [at_x(d) for d in reversed(XS)]
        + [above, below]
    )
    for peer in peers:
        pl.semaphore_signal(barrier, inc=1, device_id=peer, device_id_type=MESH)
    part = NZ_CHIPS * ROWS

    def part_of(at):
        return pl.ds(pl.multiple_of(at * part, part), part)

    def pack_gauges():
        owners = owner[...]
        member = jnp.where(iota((NGY, COLS), 0) == owners, 1.0, 0.0).astype(f32)
        upper = jnp.where(iota((COLS, COLS), 0) <= iota((COLS, COLS), 1), 1.0, 0.0).astype(bf16)
        counted = dot(member.astype(bf16), upper)
        rank = jnp.sum(counted * member, axis=0, keepdims=True).astype(jnp.int32) - 1
        target = owners * 16 + rank
        picked = jnp.where(iota((2 * COLS, COLS), 0) == target, 1.0, 0.0).astype(bf16)
        onehot[...] = picked
        cells = cell[...]
        row = lax.shift_right_logical(cells, 7).astype(f32)
        col = lax.bitwise_and(cells, COLS - 1).astype(f32)
        payload = jnp.concatenate([obs[...], weight[...], row, col, jnp.ones_like(row)], axis=0)
        parts = jnp.concatenate([p.astype(f32) for p in split3(payload)], axis=0).astype(bf16)
        placed = dot_nt(parts, picked)
        placed = placed[0:8] + placed[8:16] + placed[16:24]
        mod = lax.rem(gy, 8)
        for d in range(NGY):
            half = placed[:, (d // 8) * COLS : (d // 8 + 1) * COLS]
            gout[d] = pltpu.roll(half, wrap(mod - d % 8, 8) * 16, 1)

    def split_once():
        high, low = split2(line[:, part_of(x)])
        ll[0, 0:ROWS] = high
        ll[0, ROWS : 2 * ROWS] = low
        for k in range(NGY):
            at = slice(k * COLS, (k + 1) * COLS)
            high, low = split2(column[:, at].T)
            ct[at, 0:COLS] = high
            ct[at, COLS : 2 * COLS] = low
        for t in range(STEPS):
            for p, piece in enumerate(split3(traj[t, 0])):
                fields3[pl.ds((p * STEPS + t) * ROWS, ROWS)] = piece

    def send_z(s, these):
        mine = ebuf.at[s, z]
        for i in these:
            send(mine, mine, e_send.at[s], e_recv.at[s, i], at_z(RING[i]))

    def send_rims(s):
        surface = surf[...]
        turned = jnp.concatenate([surface, ebuf[s, z]], axis=0).T
        yh_out[s, 0] = turned[0:8]
        yh_out[s, 1] = turned[COLS - 8 :]
        send(yh_out.at[s, 0], yh_in.at[s, 1], yh_send.at[s], yh_recv.at[s, 1], before)
        send(yh_out.at[s, 1], yh_in.at[s, 0], yh_send.at[s], yh_recv.at[s, 0], after)

    def send_x_rims(s):
        surface = surf[...]
        north = nbuf[s, nslot]
        xh_out[s, 0, 0] = surface[0:8]
        xh_out[s, 0, 1] = north[0:8]
        xh_out[s, 1, 0] = surface[ROWS - 8 :]
        xh_out[s, 1, 1] = north[ROWS - 8 :]
        send(xh_out.at[s, 0], xh_in.at[s, 1], xh_send.at[s], xh_recv.at[s, 1], above)
        send(xh_out.at[s, 1], xh_in.at[s, 0], xh_send.at[s], xh_recv.at[s, 0], below)

    def send_y(s):
        own = nbuf.at[s, nslot]
        for i in (6, 5, 4, 3, 2, 1, 0):
            send(own, own, n_send.at[s], n_yrecv.at[s, i], at_y(RING[i]))
        send(own, own, n_send.at[s], n_crecv.at[s], sibling)

    def start_once():
        loads[5].wait()
        for j, d in enumerate(XS):
            piece = line.at[:, part_of(wrap(x + d, NX_CHIPS))]
            send(piece, lpart.at[j], l_send.at[0], l_recv.at[0, j], at_x(d))
        send(line.at[pl.ds(0, 8)], lrim.at[1], once_send.at[3], once_recv.at[5], above)
        send(line.at[pl.ds(ROWS - 8, 8)], lrim.at[0], once_send.at[3], once_recv.at[6], below)
        for i in (3, 4, 6, 7, 8, 9, 10):
            loads[i].wait()
        send(column.at[pl.ds(0, 8)], crim.at[1], once_send.at[4], once_recv.at[7], before)
        send(column.at[pl.ds(COLS - 8, 8)], crim.at[0], once_send.at[4], once_recv.at[8], after)
        pack_gauges()
        gin[gy] = gout[gy]
        for d in range(1, NGY):
            peer = lax.rem(gy + d, NGY)
            send(gout.at[peer], gin.at[gy], once_send.at[2], once_recv.at[4], (gx, peer))
        both = pl.ds(1, 2)
        send(traj.at[:, both, pl.ds(0, 8)], tx_in.at[1], once_send.at[0], once_recv.at[0], above)
        send(
            traj.at[:, both, pl.ds(ROWS - 8, 8)],
            tx_in.at[0],
            once_send.at[0],
            once_recv.at[1],
            below,
        )
        for t in range(STEPS):
            turned = jnp.concatenate([traj[t, 1], traj[t, 2]], axis=0).T
            ty_out[0, t] = turned[0:8]
            ty_out[1, t] = turned[COLS - 8 :]
        send(ty_out.at[0], ty_in.at[1], once_send.at[1], once_recv.at[2], before)
        send(ty_out.at[1], ty_in.at[0], once_send.at[1], once_recv.at[3], after)

    def gauges():
        arrive(gin.at[pl.ds(0, NGY - 1)], once_recv.at[4])
        mod = lax.rem(gy, 8)
        lane8 = iota((8, COLS), 1)
        total = None
        for half in range(2):
            record = gin[half * 8]
            for k in range(1, 8):
                record = jnp.where(lax.shift_right_logical(lane8, 4) == k, gin[half * 8 + k], record)
            valid = record[7:8] > 0.5
            row = record[5:6].astype(jnp.int32)
            col = record[6:7].astype(jnp.int32)
            in_col = jnp.where((iota((COLS, COLS), 0) == col) & valid, 1.0, 0.0).astype(bf16)
            in_row = jnp.where(iota((ROWS, COLS), 0) == row, 1.0, 0.0).astype(f32)
            seen = dot(fields3[...], in_col)
            misfits, parts = [], [[], [], []]
            for t in range(STEPS):
                at = [seen[(p * STEPS + t) * ROWS : (p * STEPS + t + 1) * ROWS] for p in range(3)]
                value = jnp.sum((at[0] + at[1] + at[2]) * in_row, axis=0, keepdims=True)
                misfit = jnp.where(valid, value - record[t : t + 1], 0.0)
                misfits.append(misfit)
                for p, piece in enumerate(split3(record[4:5] * misfit)):
                    parts[p].append((in_row * piece.astype(f32)).astype(bf16))
            back = jnp.concatenate(misfits + [jnp.zeros((4, COLS), f32)], axis=0)
            for k in range(8):
                rout[half * 8 + k] = pltpu.roll(back, wrap(mod - k, 8) * 16, 1)
            spread = dot_nt(jnp.concatenate(parts[0] + parts[1] + parts[2], axis=0), in_col)
            total = spread if total is None else total + spread
        size = STEPS * ROWS
        total = total[0:size] + total[size : 2 * size] + total[2 * size :]
        for t in range(STEPS):
            forcing[t] = total[t * ROWS : (t + 1) * ROWS]
        rin[gy] = rout[gy]
        for d in range(1, NGY):
            peer = lax.rem(gy + d, NGY)
            send(rout.at[peer], rin.at[gy], once_send.at[5], once_recv.at[9], (gx, peer))

    def pass_rims():
        arrive(lrim.at[0], once_recv.at[5])
        arrive(lrim.at[0], once_recv.at[6])
        lmerged[...] = merge_x(lrim[0], lrim[1])
        for j, d in enumerate(XS):
            piece = lmerged.at[:, part_of(wrap(x + d, NX_CHIPS))]
            send(piece, lrimpart.at[j], l_send.at[1], l_recv.at[1, j], at_x(d))

    def both_parts(rim):
        high = rim.astype(bf16).astype(f32)
        return jnp.concatenate([high, rim - high], axis=0).astype(bf16)

    def prepare():
        ll[0, 2 * ROWS :] = both_parts(lmerged[:, part_of(x)])
        for j in range(3):
            arrive(lpart.at[j], l_recv.at[0, j])
            high, low = split2(lpart[j])
            ll[1 + j, 0:ROWS] = high
            ll[1 + j, ROWS : 2 * ROWS] = low
            arrive(lrimpart.at[j], l_recv.at[1, j])
            ll[1 + j, 2 * ROWS :] = both_parts(lrimpart[j])

    def prepare_column():
        arrive(crim.at[0], once_recv.at[7])
        arrive(crim.at[0], once_recv.at[8])
        cx[...] = both_parts(merge_y(crim[0], crim[1]))

    def spread_y(merged):
        return jnp.concatenate([merged, jnp.zeros((COLS - 16, COLS), f32), merged], axis=0).T

    def rim_y(left, right):
        return spread_y(merge_y(left, right))

    def step(s, carry):
        t = STEPS - 1 - s
        def keep(at, block):
            high, low = split2(block)
            rows = pl.ds(pl.multiple_of(at * ROWS, ROWS), ROWS)
            ez[rows, 0:COLS] = high
            ez[rows, COLS : 2 * COLS] = low

        def from_z(i):
            at = wrap(z - RING[i], NZ_CHIPS)
            arrive(ebuf.at[s, at], e_recv.at[s, i])
            keep(at, ebuf[s, at])

        def from_y(i):
            block = nbuf.at[s, core * NY_CHIPS + wrap(y - RING[i], NY_CHIPS)]
            arrive(block, n_yrecv.at[s, i])
            send(block, block, n_send.at[s], n_crecv.at[s], sibling)

        keep(z, ebuf[s, z])
        arrive(yh_in.at[s, 0], yh_recv.at[s, 0])
        arrive(yh_in.at[s, 0], yh_recv.at[s, 1])
        eedge[s, z] = merge_y(yh_in[s, 0], yh_in[s, 1])
        for d in RING:
            send(eedge.at[s, z], eedge.at[s, z], ee_send.at[s], ee_recv.at[s], at_z(d))
        arrive(xh_in.at[s, 0], xh_recv.at[s, 0])
        arrive(xh_in.at[s, 1], xh_recv.at[s, 1])
        nedge[s, nslot] = merge_x(xh_in[s, 0, 1], xh_in[s, 1, 1])
        for d in RING:
            send(nedge.at[s, nslot], nedge.at[s, nslot], ne_send.at[s], ne_recv.at[s, 0], at_y(d))
        from_y(0)
        from_y(1)
        from_z(0)
        from_z(1)
        from_y(2)
        from_y(3)
        from_z(2)
        from_z(3)

        @pl.when(s == 0)
        def _():
            pass_rims()
            split_once()

        from_z(4)
        from_z(5)
        from_z(6)

        @pl.when(s == 0)
        def _():
            prepare()

        def line_share(slot):
            product = dot(ll[slot], ez[...])
            inner, rim = joined(product)
            return inner, rim, dot_nt(ae[...], ll[slot, 0 : 2 * ROWS, :])

        def joined(product):
            left, right = product[:, 0:COLS], product[:, COLS:]
            inner = left[0:ROWS] + (right[0:ROWS] + left[ROWS : 2 * ROWS])
            at = 2 * ROWS
            rim = left[at : at + 8] + (right[at : at + 8] + left[at + 8 : at + 16])
            return inner, rim

        def turned_rim(product):
            return product[0:8] + (pltpu.roll(product[0:8], ROWS, 1) + product[8:16])

        arrive(eedge.at[s, pl.ds(0, NZ_CHIPS - 1)], ee_recv.at[s])
        lane = iota((8, COLS), 1)
        for k in range(NZ_CHIPS // 2):
            rim = jnp.where(lane < ROWS, pltpu.roll(eedge[s, 2 * k], ROWS, 1), eedge[s, 2 * k + 1])
            ae[:, k * COLS : (k + 1) * COLS] = both_parts(rim)
        for j in (2, 0, 1):
            inner, rim, sides = line_share(1 + j)
            pout[s, j, 0:ROWS] = inner
            pout[s, j, ROWS : ROWS + 8] = rim
            pout[s, j, ROWS + 8 : ROWS + 16] = turned_rim(sides)
            send(pout.at[s, j], pin.at[s, j], p_send.at[s], p_recv.at[s, j], at_x(-XS[j]))
        from_y(4)
        from_y(5)
        from_y(6)
        arrive(nedge.at[s, pl.ds(0, NY_CHIPS - 1)], ne_recv.at[s, 0])
        column_edges = nedge.at[s, pl.ds(core * NY_CHIPS, NY_CHIPS)]
        send(column_edges, column_edges, ne_send.at[s], ne_recv.at[s, 1], sibling)
        line_adjoint, line_x, sides = line_share(0)
        line_y = turned_rim(sides)

        @pl.when(s == 0)
        def _():
            arrive(tx_in.at[0], once_recv.at[0])
            arrive(tx_in.at[0], once_recv.at[1])
            arrive(ty_in.at[0], once_recv.at[2])
            arrive(ty_in.at[0], once_recv.at[3])
            prepare_column()
            gauges()

        surface = surf[...]
        east, north = traj[t, 1], traj[t, 2]
        whole = depth[...] + traj[t, 0]
        rim_surface = rim_y(yh_in[s, 0], yh_in[s, 1])[0:ROWS]
        flux_x = mass_rate * slope_x(surface, merge_x(xh_in[s, 0, 0], xh_in[s, 1, 0]))
        flux_y = mass_rate * slope_y(surface, rim_surface)
        gain = east * flux_x + north * flux_y
        depth_out[...] = jnp.where(s == 0, 0.0, depth_out[...]) + gain
        base[0] = surface + gain
        base[1] = whole * flux_x
        base[2] = whole * flux_y
        rims = rim_y(ty_in[0, t], ty_in[1, t])
        east_x = merge_x(tx_in[0, t, 0], tx_in[1, t, 0])
        north_x = merge_x(tx_in[0, t, 1], tx_in[1, t, 1])
        north_y = rims[ROWS:]
        coef[0] = 1.0 - advect_rate * slope_x(east, east_x)
        coef[1] = advect_rate * slope_x(north, north_x)
        coef[2] = advect_rate * slope_y(east, rims[0:ROWS])
        coef[3] = 1.0 - advect_rate * slope_y(north, north_y)

        arrive(nbuf.at[s, pl.ds(0, NY_CHIPS)], n_crecv.at[s])
        arrive(nedge.at[s, pl.ds(0, NY_CHIPS)], ne_recv.at[s, 1])
        for k in range(NGY):
            at = ((k % NY_CHIPS) * 2 + k // NY_CHIPS) * COLS
            at = slice(at, at + COLS)
            high, low = split2(nbuf[s, k])
            nn[0:ROWS, at] = high
            nn[ROWS : 2 * ROWS, at] = low
            nn[2 * ROWS : 2 * ROWS + 16, at] = both_parts(nedge[s, k])
        column_adjoint, column_x = joined(dot(nn[...], ct[...]))
        column_y = spread_y(turned_rim(dot_nt(cx[...], nn[0 : 2 * ROWS, :])))[0:ROWS]

        for j in range(3):
            arrive(pin.at[s, j], p_recv.at[s, j])
            line_adjoint += pin[s, j, 0:ROWS]
            line_x += pin[s, j, ROWS : ROWS + 8]
            line_y += pin[s, j, ROWS + 8 : ROWS + 16]
        line_y = spread_y(line_y)[0:ROWS]

        along_x = slope_x(line_adjoint, line_x)
        along_y = slope_y(column_adjoint, column_y)
        mixed = slope_x(east * line_adjoint, east_x * line_x) + slope_y(
            north * line_adjoint, north_y * line_y
        )
        ebuf[s + 1, z] = (
            line_adjoint * coef[0] - column_adjoint * coef[1] + advect_rate * mixed + base[1]
        )

        surf[...] = base[0] + forcing[t] + slope_rate * (along_x + along_y)
        mixed = slope_x(east * column_adjoint, east_x * column_x) + slope_y(
            north * column_adjoint, north_y * column_y
        )
        nbuf[s + 1, nslot] = (
            column_adjoint * coef[3] - line_adjoint * coef[2] + advect_rate * mixed + base[2]
        )

        @pl.when(s < STEPS - 1)
        def _():
            send_rims(s + 1)
            send_x_rims(s + 1)
            send_z(s + 1, (6, 5, 4, 3, 2, 1, 0))
            send_y(s + 1)

        return carry

    for i in range(3):
        loads[i].wait()
    pl.semaphore_wait(barrier, len(peers))
    send_rims(0)
    send_x_rims(0)
    send_z(0, (6, 5, 4, 3, 2, 1, 0))
    send_y(0)
    start_once()
    lax.fori_loop(0, STEPS, step, 0)

    state_out[0] = surf[...]
    state_out[1] = ebuf[STEPS, z]
    state_out[2] = nbuf[STEPS, nslot]

    arrive(rin.at[pl.ds(0, NGY - 1)], once_recv.at[9])
    lane8 = iota((8, COLS), 1)
    halves = []
    for half in range(2):
        record = rin[half * 8]
        for k in range(1, 8):
            record = jnp.where(lax.shift_right_logical(lane8, 4) == k, rin[half * 8 + k], record)
        halves.append(record)
    returned = jnp.concatenate(halves, axis=1)
    pieces = jnp.concatenate([p.astype(f32) for p in split3(returned)], axis=0).astype(bf16)
    found = dot(pieces, onehot[...])
    residual_out[...] = found[0:4] + found[8:12] + found[16:20]
    for s in range(STEPS):
        arrive(ebuf.at[s, pl.ds(0, NZ_CHIPS - 1)], e_send.at[s])
        arrive(pout.at[s], p_send.at[s])
        arrive(nbuf.at[s, pl.ds(0, NGY - 1)], n_send.at[s])
        arrive(eedge.at[s, pl.ds(0, NZ_CHIPS - 1)], ee_send.at[s])
        arrive(nedge.at[s, pl.ds(0, NGY - 1)], ne_send.at[s])
        arrive(xh_out.at[s], xh_send.at[s])
        arrive(yh_out.at[s], yh_send.at[s])
    arrive(lpart, l_send.at[0])
    arrive(lrimpart, l_send.at[1])
    arrive(tx_in, once_send.at[0])
    arrive(ty_out, once_send.at[1])
    arrive(gout.at[pl.ds(0, NGY - 1)], once_send.at[2])
    arrive(lrim, once_send.at[3])
    arrive(crim, once_send.at[4])
    arrive(rout.at[pl.ds(0, NGY - 1)], once_send.at[5])


def hand_over(state_in, depth_in, residual_in, state_out, depth_out, residual_out):
    state_out[...] = state_in[...]
    depth_out[...] = depth_in[...]
    residual_out[...] = residual_in[...]


def per_device(
    trajectory,
    depth,
    cotangent,
    line_inverse,
    column_inverse,
    gauge_owner,
    gauge_cell,
    gauge_obs,
    gauge_weight,
):
    vmem = pltpu.VMEM
    dma = pltpu.SemaphoreType.DMA
    scratch = [
        vmem((STEPS, 3, ROWS, COLS), f32),
        vmem((ROWS, COLS), f32),
        vmem((ROWS, 2048), f32),
        vmem((COLS, 2048), f32),
        vmem((1, COLS), jnp.int32),
        vmem((1, COLS), jnp.int32),
        vmem((STEPS, COLS), f32),
        vmem((1, COLS), f32),
        vmem((ROWS, COLS), f32),
        vmem((STEPS + 1, NZ_CHIPS, ROWS, COLS), f32),
        vmem((STEPS + 1, NGY, ROWS, COLS), f32),
        vmem((STEPS, NZ_CHIPS, 8, COLS), f32),
        vmem((STEPS, NGY, 8, COLS), f32),
        vmem((STEPS, 2, 2, 8, COLS), f32),
        vmem((STEPS, 2, 2, 8, COLS), f32),
        vmem((STEPS, 2, 8, COLS), f32),
        vmem((STEPS, 2, 8, COLS), f32),
        vmem((2, 8, 2048), f32),
        vmem((2, 8, 2048), f32),
        vmem((2, STEPS, 2, 8, COLS), f32),
        vmem((2, STEPS, 8, COLS), f32),
        vmem((2, STEPS, 8, COLS), f32),
        vmem((NGY, 8, COLS), f32),
        vmem((NGY, 8, COLS), f32),
        vmem((NGY, 8, COLS), f32),
        vmem((NGY, 8, COLS), f32),
        vmem((3, ROWS, 512), f32),
        vmem((3, 8, 512), f32),
        vmem((8, 2048), f32),
        vmem((STEPS, 3, ROWS + 16, COLS), f32),
        vmem((STEPS, 3, ROWS + 16, COLS), f32),
        vmem((2 * COLS, COLS), bf16),
        vmem((4, 2 * ROWS + 16, 512), bf16),
        vmem((2048, 2 * COLS), bf16),
        vmem((16, 2048), bf16),
        vmem((2 * ROWS + 16, 2048), bf16),
        vmem((16, 512), bf16),
        vmem((512, 2 * COLS), bf16),
        vmem((3 * STEPS * ROWS, COLS), bf16),
        vmem((STEPS, ROWS, COLS), f32),
        vmem((3, ROWS, COLS), f32),
        vmem((4, ROWS, COLS), f32),
        dma((11,)),
        dma((STEPS,)),
        dma((STEPS, 7)),
        dma((STEPS,)),
        dma((STEPS, 3)),
        dma((STEPS,)),
        dma((STEPS, 7)),
        dma((STEPS,)),
        dma((STEPS,)),
        dma((STEPS,)),
        dma((STEPS,)),
        dma((STEPS, 2)),
        dma((STEPS,)),
        dma((STEPS, 2)),
        dma((STEPS,)),
        dma((STEPS, 2)),
        dma((2,)),
        dma((2, 3)),
        dma((6,)),
        dma((10,)),
    ]
    anywhere = pl.BlockSpec(memory_space=pl.ANY)
    here = pl.BlockSpec(memory_space=pltpu.VMEM)
    results = pl.pallas_call(
        kernel,
        name="adjoint",
        out_shape=(
            jax.ShapeDtypeStruct((3, ROWS, COLS), f32),
            jax.ShapeDtypeStruct((ROWS, COLS), f32),
            jax.ShapeDtypeStruct((STEPS, COLS), f32),
        ),
        in_specs=[anywhere] * 9,
        out_specs=(here, here, here),
        scratch_shapes=scratch,
        compiler_params=pltpu.CompilerParams(
            collective_id=0, has_side_effects=True, vmem_limit_bytes=60 * 2**20
        ),
    )(
        trajectory,
        depth,
        cotangent,
        line_inverse,
        column_inverse,
        gauge_owner.reshape(1, COLS),
        gauge_cell.reshape(1, COLS),
        gauge_obs,
        gauge_weight.reshape(1, COLS),
    )
    return pl.pallas_call(
        hand_over,
        name="hand_over",
        out_shape=tuple(jax.ShapeDtypeStruct(r.shape, r.dtype) for r in results),
        in_specs=[here] * 3,
        out_specs=(here, here, here),
    )(*results)


def solution(mesh):
    return jax.shard_map(
        per_device,
        mesh=mesh,
        in_specs=(
            P(None, None, "gx", "gy"),
            P("gx", "gy"),
            P(None, "gx", "gy"),
            P("gx", None),
            P("gy", None),
            P(("gx", "gy"), None),
            P(("gx", "gy")),
            P(None, ("gx", "gy")),
            P(("gx", "gy")),
        ),
        out_specs=(P(None, "gx", "gy"), P("gx", "gy"), P(None, ("gx", "gy"))),
        check_vma=False,
    )
```

time: 102 us -> 77.9 us (0.76); the launches traced: 101 us -> 77.8 us
  Pallas kernels: 92.7 us -> 77.1 us
  local copies, waits for them, and re-layouts: 7.42 us -> 0 us
    pallas_call x1, Pallas kernels: 92.7 us -> 75.5 us  [per_device(): pl.pallas_call(kernel, name='adjoint', out_shape=(jax.ShapeDtypeStruct((3...]
    unnamed x21 -> x0, local copies, waits for them, and re-layouts: 7.42 us -> none
    pallas_call x0 -> x1, Pallas kernels: none -> 1.57 us  [per_device(): pl.pallas_call(hand_over, name='hand_over', out_shape=tuple((jax.ShapeDty...]
where the time goes in v2:
time: 77.9 us; the launch traced here: 77.8 us
  Pallas kernels  77.1 us (99%)
    pallas_call x1, Pallas kernels, per_device(): pl.pallas_call(kernel, name='adjoint', out_shape=(jax.ShapeDtypeStruct((3...  75.5 us
    pallas_call x1, Pallas kernels, per_device(): pl.pallas_call(hand_over, name='hand_over', out_shape=tuple((jax.ShapeDty...  1.57 us

profile of v2, /device:TPU:1, one launch (start us, length us, event | category | flops | bytes accessed | tf_op | source)
XLA Modules:
  0.0 77.8 jit_solution(2538301425147075949)
XLA Ops:
  0.6 75.5 %adjoint.1 = (f32[3,64,128]{2,1,0:T(8,128)}, f32[64,128]{1,0:T(8,128)}, f32[4,128]{1,0:T(4,128)}) custom-call(f32[4,3,64,128]{3,2,1,0:T(8,128)} %traj_in.1, f32[64,128]{1,0:T(8,128)} %depth_in.1, f32[3,64,128]{2,1,0:T(8,128)} %cot_in.1, f32[64,2048]{1,0:T(8,128)} %line_in.1, f32[128,2048]{1,0:T(8,128)} %column_in.1, s32[1,128]{1,0:T(1,128)} %bitcast.3, ...), custom_call_target="tpu_custom_call" | custom-call | tf_op jit(solution)/shard_map/adjoint/pallas_call | solution.py:683
  76.2 1.6 %hand_over.1 = (f32[3,64,128]{2,1,0:T(8,128)}, f32[64,128]{1,0:T(8,128)}, f32[4,128]{1,0:T(4,128)}) custom-call(f32[3,64,128]{2,1,0:T(8,128)} %get-tuple-element.6.state_in, f32[64,128]{1,0:T(8,128)} %get-tuple-element.7.depth_in, f32[4,128]{1,0:T(4,128)} %get-tuple-element.8.residual_in), custom_call_target="tpu_custom_call" | custom-call | tf_op jit(solution)/shard_map/hand_over/pallas_call | solution.py:708

commit v3 on v2

--- a/solution.py
+++ b/solution.py
@@ -116,6 +116,8 @@
     lmerged,
     pout,
     pin,
+    qout,
+    qin,
     onehot,
     ll,
     ct,
@@ -132,6 +134,8 @@
     e_recv,
     p_send,
     p_recv,
+    q_send,
+    q_recv,
     n_send,
     n_yrecv,
     n_crecv,
@@ -209,8 +213,6 @@
             ]
         )
     ]
-    for copy in loads:
-        copy.start()
 
     barrier = pltpu.get_barrier_semaphore()
     peers = (
@@ -221,6 +223,8 @@
     )
     for peer in peers:
         pl.semaphore_signal(barrier, inc=1, device_id=peer, device_id_type=MESH)
+    for copy in loads:
+        copy.start()
     part = NZ_CHIPS * ROWS
 
     def part_of(at):
@@ -290,12 +294,9 @@
         send(own, own, n_send.at[s], n_crecv.at[s], sibling)
 
     def start_once():
-        loads[5].wait()
         for j, d in enumerate(XS):
             piece = line.at[:, part_of(wrap(x + d, NX_CHIPS))]
             send(piece, lpart.at[j], l_send.at[0], l_recv.at[0, j], at_x(d))
-        send(line.at[pl.ds(0, 8)], lrim.at[1], once_send.at[3], once_recv.at[5], above)
-        send(line.at[pl.ds(ROWS - 8, 8)], lrim.at[0], once_send.at[3], once_recv.at[6], below)
         for i in (3, 4, 6, 7, 8, 9, 10):
             loads[i].wait()
         send(column.at[pl.ds(0, 8)], crim.at[1], once_send.at[4], once_recv.at[7], before)
@@ -371,12 +372,15 @@
         return jnp.concatenate([high, rim - high], axis=0).astype(bf16)
 
     def prepare():
-        ll[0, 2 * ROWS :] = both_parts(lmerged[:, part_of(x)])
         for j in range(3):
             arrive(lpart.at[j], l_recv.at[0, j])
             high, low = split2(lpart[j])
             ll[1 + j, 0:ROWS] = high
             ll[1 + j, ROWS : 2 * ROWS] = low
+
+    def prepare_rims():
+        ll[0, 2 * ROWS :] = both_parts(lmerged[:, part_of(x)])
+        for j in range(3):
             arrive(lrimpart.at[j], l_recv.at[1, j])
             ll[1 + j, 2 * ROWS :] = both_parts(lrimpart[j])
 
@@ -390,6 +394,40 @@
 
     def rim_y(left, right):
         return spread_y(merge_y(left, right))
+
+    def residuals():
+        arrive(rin.at[pl.ds(0, NGY - 1)], once_recv.at[9])
+        lane8 = iota((8, COLS), 1)
+        halves = []
+        for half in range(2):
+            record = rin[half * 8]
+            for k in range(1, 8):
+                record = jnp.where(lax.shift_right_logical(lane8, 4) == k, rin[half * 8 + k], record)
+            halves.append(record)
+        returned = jnp.concatenate(halves, axis=1)
+        pieces = jnp.concatenate([p.astype(f32) for p in split3(returned)], axis=0).astype(bf16)
+        found = dot(pieces, onehot[...])
+        residual_out[...] = found[0:4] + found[8:12] + found[16:20]
+
+    def left_step(s):
+        arrive(ebuf.at[s, pl.ds(0, NZ_CHIPS - 1)], e_send.at[s])
+        arrive(pout.at[s], p_send.at[s])
+        arrive(qout.at[s], q_send.at[s])
+        arrive(nbuf.at[s, pl.ds(0, NGY - 1)], n_send.at[s])
+        arrive(eedge.at[s, pl.ds(0, NZ_CHIPS - 1)], ee_send.at[s])
+        arrive(nedge.at[s, pl.ds(0, NGY - 1)], ne_send.at[s])
+        arrive(xh_out.at[s], xh_send.at[s])
+        arrive(yh_out.at[s], yh_send.at[s])
+
+    def left_once():
+        arrive(lpart, l_send.at[0])
+        arrive(lrimpart, l_send.at[1])
+        arrive(tx_in, once_send.at[0])
+        arrive(ty_out, once_send.at[1])
+        arrive(gout.at[pl.ds(0, NGY - 1)], once_send.at[2])
+        arrive(lrim, once_send.at[3])
+        arrive(crim, once_send.at[4])
+        arrive(rout.at[pl.ds(0, NGY - 1)], once_send.at[5])
 
     def step(s, carry):
         t = STEPS - 1 - s
@@ -420,6 +458,11 @@
         nedge[s, nslot] = merge_x(xh_in[s, 0, 1], xh_in[s, 1, 1])
         for d in RING:
             send(nedge.at[s, nslot], nedge.at[s, nslot], ne_send.at[s], ne_recv.at[s, 0], at_y(d))
+
+        @pl.when(s == 0)
+        def _():
+            pass_rims()
+
         from_y(0)
         from_y(1)
         from_z(0)
@@ -431,7 +474,6 @@
 
         @pl.when(s == 0)
         def _():
-            pass_rims()
             split_once()
 
         from_z(4)
@@ -442,20 +484,33 @@
         def _():
             prepare()
 
+        def side_share(slot):
+            return turned_rim(dot_nt(ae[...], ll[slot, 0 : 2 * ROWS, :]))
+
         def line_share(slot):
-            product = dot(ll[slot], ez[...])
-            inner, rim = joined(product)
-            return inner, rim, dot_nt(ae[...], ll[slot, 0 : 2 * ROWS, :])
-
-        def joined(product):
+            return dot(ll[slot, 0 : 2 * ROWS], ez[...])
+
+        def rim_share(slot):
+            return dot(ll[slot, 2 * ROWS :], ez[...])
+
+        def inner_of(product):
             left, right = product[:, 0:COLS], product[:, COLS:]
-            inner = left[0:ROWS] + (right[0:ROWS] + left[ROWS : 2 * ROWS])
-            at = 2 * ROWS
-            rim = left[at : at + 8] + (right[at : at + 8] + left[at + 8 : at + 16])
-            return inner, rim
+            return left[0:ROWS] + (right[0:ROWS] + left[ROWS : 2 * ROWS])
+
+        def rim_of(product, at):
+            left, right = product[:, 0:COLS], product[:, COLS:]
+            return left[at : at + 8] + (right[at : at + 8] + left[at + 8 : at + 16])
 
         def turned_rim(product):
             return product[0:8] + (pltpu.roll(product[0:8], ROWS, 1) + product[8:16])
+
+        for j in (2, 0, 1):
+            pout[s, j] = inner_of(line_share(1 + j))
+            send(pout.at[s, j], pin.at[s, j], p_send.at[s], p_recv.at[s, j], at_x(-XS[j]))
+
+        @pl.when(s == 0)
+        def _():
+            prepare_rims()
 
         arrive(eedge.at[s, pl.ds(0, NZ_CHIPS - 1)], ee_recv.at[s])
         lane = iota((8, COLS), 1)
@@ -463,19 +518,18 @@
             rim = jnp.where(lane < ROWS, pltpu.roll(eedge[s, 2 * k], ROWS, 1), eedge[s, 2 * k + 1])
             ae[:, k * COLS : (k + 1) * COLS] = both_parts(rim)
         for j in (2, 0, 1):
-            inner, rim, sides = line_share(1 + j)
-            pout[s, j, 0:ROWS] = inner
-            pout[s, j, ROWS : ROWS + 8] = rim
-            pout[s, j, ROWS + 8 : ROWS + 16] = turned_rim(sides)
-            send(pout.at[s, j], pin.at[s, j], p_send.at[s], p_recv.at[s, j], at_x(-XS[j]))
+            qout[s, j, 0:8] = rim_of(rim_share(1 + j), 0)
+            qout[s, j, 8:16] = side_share(1 + j)
+            send(qout.at[s, j], qin.at[s, j], q_send.at[s], q_recv.at[s, j], at_x(-XS[j]))
         from_y(4)
         from_y(5)
         from_y(6)
         arrive(nedge.at[s, pl.ds(0, NY_CHIPS - 1)], ne_recv.at[s, 0])
         column_edges = nedge.at[s, pl.ds(core * NY_CHIPS, NY_CHIPS)]
         send(column_edges, column_edges, ne_send.at[s], ne_recv.at[s, 1], sibling)
-        line_adjoint, line_x, sides = line_share(0)
-        line_y = turned_rim(sides)
+        line_adjoint = inner_of(line_share(0))
+        line_x = rim_of(rim_share(0), 0)
+        line_y = side_share(0)
 
         @pl.when(s == 0)
         def _():
@@ -515,15 +569,27 @@
             nn[0:ROWS, at] = high
             nn[ROWS : 2 * ROWS, at] = low
             nn[2 * ROWS : 2 * ROWS + 16, at] = both_parts(nedge[s, k])
-        column_adjoint, column_x = joined(dot(nn[...], ct[...]))
+        product = dot(nn[...], ct[...])
+        column_adjoint, column_x = inner_of(product), rim_of(product, 2 * ROWS)
         column_y = spread_y(turned_rim(dot_nt(cx[...], nn[0 : 2 * ROWS, :])))[0:ROWS]
 
+        @pl.when(s > 0)
+        def _():
+            left_step(s - 1)
+
+        @pl.when(s == 2)
+        def _():
+            residuals()
+            left_once()
+
+        for j in range(3):
+            arrive(qin.at[s, j], q_recv.at[s, j])
+            line_x += qin[s, j, 0:8]
+            line_y += qin[s, j, 8:16]
+        line_y = spread_y(line_y)[0:ROWS]
         for j in range(3):
             arrive(pin.at[s, j], p_recv.at[s, j])
-            line_adjoint += pin[s, j, 0:ROWS]
-            line_x += pin[s, j, ROWS : ROWS + 8]
-            line_y += pin[s, j, ROWS + 8 : ROWS + 16]
-        line_y = spread_y(line_y)[0:ROWS]
+            line_adjoint += pin[s, j]
 
         along_x = slope_x(line_adjoint, line_x)
         along_y = slope_y(column_adjoint, column_y)
@@ -544,9 +610,9 @@
 
         @pl.when(s < STEPS - 1)
         def _():
-            send_rims(s + 1)
             send_x_rims(s + 1)
             send_z(s + 1, (6, 5, 4, 3, 2, 1, 0))
+            send_rims(s + 1)
             send_y(s + 1)
 
         return carry
@@ -554,9 +620,12 @@
     for i in range(3):
         loads[i].wait()
     pl.semaphore_wait(barrier, len(peers))
+    send_x_rims(0)
+    loads[5].wait()
+    send(line.at[pl.ds(0, 8)], lrim.at[1], once_send.at[3], once_recv.at[5], above)
+    send(line.at[pl.ds(ROWS - 8, 8)], lrim.at[0], once_send.at[3], once_recv.at[6], below)
+    send_z(0, (6, 5, 4, 3, 2, 1, 0))
     send_rims(0)
-    send_x_rims(0)
-    send_z(0, (6, 5, 4, 3, 2, 1, 0))
     send_y(0)
     start_once()
     lax.fori_loop(0, STEPS, step, 0)
@@ -565,34 +634,7 @@
     state_out[1] = ebuf[STEPS, z]
     state_out[2] = nbuf[STEPS, nslot]
 
-    arrive(rin.at[pl.ds(0, NGY - 1)], once_recv.at[9])
-    lane8 = iota((8, COLS), 1)
-    halves = []
-    for half in range(2):
-        record = rin[half * 8]
-        for k in range(1, 8):
-            record = jnp.where(lax.shift_right_logical(lane8, 4) == k, rin[half * 8 + k], record)
-        halves.append(record)
-    returned = jnp.concatenate(halves, axis=1)
-    pieces = jnp.concatenate([p.astype(f32) for p in split3(returned)], axis=0).astype(bf16)
-    found = dot(pieces, onehot[...])
-    residual_out[...] = found[0:4] + found[8:12] + found[16:20]
-    for s in range(STEPS):
-        arrive(ebuf.at[s, pl.ds(0, NZ_CHIPS - 1)], e_send.at[s])
-        arrive(pout.at[s], p_send.at[s])
-        arrive(nbuf.at[s, pl.ds(0, NGY - 1)], n_send.at[s])
-        arrive(eedge.at[s, pl.ds(0, NZ_CHIPS - 1)], ee_send.at[s])
-        arrive(nedge.at[s, pl.ds(0, NGY - 1)], ne_send.at[s])
-        arrive(xh_out.at[s], xh_send.at[s])
-        arrive(yh_out.at[s], yh_send.at[s])
-    arrive(lpart, l_send.at[0])
-    arrive(lrimpart, l_send.at[1])
-    arrive(tx_in, once_send.at[0])
-    arrive(ty_out, once_send.at[1])
-    arrive(gout.at[pl.ds(0, NGY - 1)], once_send.at[2])
-    arrive(lrim, once_send.at[3])
-    arrive(crim, once_send.at[4])
-    arrive(rout.at[pl.ds(0, NGY - 1)], once_send.at[5])
+    left_step(STEPS - 1)
 
 
 def hand_over(state_in, depth_in, residual_in, state_out, depth_out, residual_out):
@@ -644,8 +686,10 @@
         vmem((3, ROWS, 512), f32),
         vmem((3, 8, 512), f32),
         vmem((8, 2048), f32),
-        vmem((STEPS, 3, ROWS + 16, COLS), f32),
-        vmem((STEPS, 3, ROWS + 16, COLS), f32),
+        vmem((STEPS, 3, ROWS, COLS), f32),
+        vmem((STEPS, 3, ROWS, COLS), f32),
+        vmem((STEPS, 3, 16, COLS), f32),
+        vmem((STEPS, 3, 16, COLS), f32),
         vmem((2 * COLS, COLS), bf16),
         vmem((4, 2 * ROWS + 16, 512), bf16),
         vmem((2048, 2 * COLS), bf16),
@@ -660,6 +704,8 @@
         dma((11,)),
         dma((STEPS,)),
         dma((STEPS, 7)),
+        dma((STEPS,)),
+        dma((STEPS, 3)),
         dma((STEPS,)),
         dma((STEPS, 3)),
         dma((STEPS,)),

time: 77.9 us -> 75.5 us (0.969)
  Pallas kernels: 77.1 us -> 74.6 us
    pallas_call x1, Pallas kernels: 75.5 us -> 73.1 us  [per_device(): pl.pallas_call(kernel, name='adjoint', out_shape=(jax.ShapeDtypeStruct((3...]
where the time goes in v3:
time: 75.5 us; the launch traced here: 75.3 us
  Pallas kernels  74.6 us (99%)
    pallas_call x1, Pallas kernels, per_device(): pl.pallas_call(kernel, name='adjoint', out_shape=(jax.ShapeDtypeStruct((3...  73.1 us
    pallas_call x1, Pallas kernels, per_device(): pl.pallas_call(hand_over, name='hand_over', out_shape=tuple((jax.ShapeDty...  1.57 us

profile of v3, /device:TPU:1, one launch (start us, length us, event | category | flops | bytes accessed | tf_op | source)
XLA Modules:
  0.0 75.3 jit_solution(9123474061812781467)
XLA Ops:
  0.6 73.1 %adjoint.1 = (f32[3,64,128]{2,1,0:T(8,128)}, f32[64,128]{1,0:T(8,128)}, f32[4,128]{1,0:T(4,128)}) custom-call(f32[4,3,64,128]{3,2,1,0:T(8,128)} %traj_in.1, f32[64,128]{1,0:T(8,128)} %depth_in.1, f32[3,64,128]{2,1,0:T(8,128)} %cot_in.1, f32[64,2048]{1,0:T(8,128)} %line_in.1, f32[128,2048]{1,0:T(8,128)} %column_in.1, s32[1,128]{1,0:T(1,128)} %bitcast.3, ...), custom_call_target="tpu_custom_call" | custom-call | tf_op jit(solution)/shard_map/adjoint/pallas_call | solution.py:729
  73.7 1.6 %hand_over.1 = (f32[3,64,128]{2,1,0:T(8,128)}, f32[64,128]{1,0:T(8,128)}, f32[4,128]{1,0:T(4,128)}) custom-call(f32[3,64,128]{2,1,0:T(8,128)} %get-tuple-element.6.state_in, f32[64,128]{1,0:T(8,128)} %get-tuple-element.7.depth_in, f32[4,128]{1,0:T(4,128)} %get-tuple-element.8.residual_in), custom_call_target="tpu_custom_call" | custom-call | tf_op jit(solution)/shard_map/hand_over/pallas_call | solution.py:754

commit v4 on v3

--- a/solution.py
+++ b/solution.py
@@ -512,13 +512,16 @@
         def _():
             prepare_rims()
 
+        for j in (2, 0, 1):
+            qout[s, j, 0:8] = rim_of(rim_share(1 + j), 0)
+        line_adjoint = inner_of(line_share(0))
+        line_x = rim_of(rim_share(0), 0)
         arrive(eedge.at[s, pl.ds(0, NZ_CHIPS - 1)], ee_recv.at[s])
         lane = iota((8, COLS), 1)
         for k in range(NZ_CHIPS // 2):
             rim = jnp.where(lane < ROWS, pltpu.roll(eedge[s, 2 * k], ROWS, 1), eedge[s, 2 * k + 1])
             ae[:, k * COLS : (k + 1) * COLS] = both_parts(rim)
         for j in (2, 0, 1):
-            qout[s, j, 0:8] = rim_of(rim_share(1 + j), 0)
             qout[s, j, 8:16] = side_share(1 + j)
             send(qout.at[s, j], qin.at[s, j], q_send.at[s], q_recv.at[s, j], at_x(-XS[j]))
         from_y(4)
@@ -527,8 +530,6 @@
         arrive(nedge.at[s, pl.ds(0, NY_CHIPS - 1)], ne_recv.at[s, 0])
         column_edges = nedge.at[s, pl.ds(core * NY_CHIPS, NY_CHIPS)]
         send(column_edges, column_edges, ne_send.at[s], ne_recv.at[s, 1], sibling)
-        line_adjoint = inner_of(line_share(0))
-        line_x = rim_of(rim_share(0), 0)
         line_y = side_share(0)
 
         @pl.when(s == 0)

time: 75.5 us -> 74.9 us (level)
  Pallas kernels: 74.6 us -> 73.8 us
    pallas_call x1, Pallas kernels: 73.1 us -> 72.2 us  [per_device(): pl.pallas_call(kernel, name='adjoint', out_shape=(jax.ShapeDtypeStruct((3...]
where the time goes in v4:
time: 74.9 us; the launch traced here: 74.4 us
  Pallas kernels  73.8 us (99%)
    pallas_call x1, Pallas kernels, per_device(): pl.pallas_call(kernel, name='adjoint', out_shape=(jax.ShapeDtypeStruct((3...  72.2 us
    pallas_call x1, Pallas kernels, per_device(): pl.pallas_call(hand_over, name='hand_over', out_shape=tuple((jax.ShapeDty...  1.57 us

profile of v4, /device:TPU:1, one launch (start us, length us, event | category | flops | bytes accessed | tf_op | source)
XLA Modules:
  0.0 74.4 jit_solution(5554832235486300585)
XLA Ops:
  0.6 72.2 %adjoint.1 = (f32[3,64,128]{2,1,0:T(8,128)}, f32[64,128]{1,0:T(8,128)}, f32[4,128]{1,0:T(4,128)}) custom-call(f32[4,3,64,128]{3,2,1,0:T(8,128)} %traj_in.1, f32[64,128]{1,0:T(8,128)} %depth_in.1, f32[3,64,128]{2,1,0:T(8,128)} %cot_in.1, f32[64,2048]{1,0:T(8,128)} %line_in.1, f32[128,2048]{1,0:T(8,128)} %column_in.1, s32[1,128]{1,0:T(1,128)} %bitcast.3, ...), custom_call_target="tpu_custom_call" | custom-call | tf_op jit(solution)/shard_map/adjoint/pallas_call | solution.py:730
  72.9 1.6 %hand_over.1 = (f32[3,64,128]{2,1,0:T(8,128)}, f32[64,128]{1,0:T(8,128)}, f32[4,128]{1,0:T(4,128)}) custom-call(f32[3,64,128]{2,1,0:T(8,128)} %get-tuple-element.6.state_in, f32[64,128]{1,0:T(8,128)} %get-tuple-element.7.depth_in, f32[4,128]{1,0:T(4,128)} %get-tuple-element.8.residual_in), custom_call_target="tpu_custom_call" | custom-call | tf_op jit(solution)/shard_map/hand_over/pallas_call | solution.py:755

commit v5 on v4

--- a/solution.py
+++ b/solution.py
@@ -221,10 +221,12 @@
         + [at_x(d) for d in reversed(XS)]
         + [above, below]
     )
+    for copy in loads[0:3]:
+        copy.start()
     for peer in peers:
         pl.semaphore_signal(barrier, inc=1, device_id=peer, device_id_type=MESH)
-    for copy in loads:
-        copy.start()
+    for i in (5, 6, 3, 4, 7, 8, 9, 10):
+        loads[i].start()
     part = NZ_CHIPS * ROWS
 
     def part_of(at):
@@ -289,7 +291,7 @@
 
     def send_y(s):
         own = nbuf.at[s, nslot]
-        for i in (6, 5, 4, 3, 2, 1, 0):
+        for i in (4, 5, 6, 2, 3, 0, 1):
             send(own, own, n_send.at[s], n_yrecv.at[s, i], at_y(RING[i]))
         send(own, own, n_send.at[s], n_crecv.at[s], sibling)
 
@@ -612,7 +614,7 @@
         @pl.when(s < STEPS - 1)
         def _():
             send_x_rims(s + 1)
-            send_z(s + 1, (6, 5, 4, 3, 2, 1, 0))
+            send_z(s + 1, (6, 4, 5, 0, 1, 2, 3))
             send_rims(s + 1)
             send_y(s + 1)
 
@@ -625,7 +627,7 @@
     loads[5].wait()
     send(line.at[pl.ds(0, 8)], lrim.at[1], once_send.at[3], once_recv.at[5], above)
     send(line.at[pl.ds(ROWS - 8, 8)], lrim.at[0], once_send.at[3], once_recv.at[6], below)
-    send_z(0, (6, 5, 4, 3, 2, 1, 0))
+    send_z(0, (6, 4, 5, 0, 1, 2, 3))
     send_rims(0)
     send_y(0)
     start_once()

time: 74.9 us -> 75.2 us (level)
  no operation moved by 1% of the time
where the time goes in v5:
time: 75.2 us; the launch traced here: 75 us
  Pallas kernels  74.4 us (99%)
    pallas_call x1, Pallas kernels, per_device(): pl.pallas_call(kernel, name='adjoint', out_shape=(jax.ShapeDtypeStruct((3...  72.8 us
    pallas_call x1, Pallas kernels, per_device(): pl.pallas_call(hand_over, name='hand_over', out_shape=tuple((jax.ShapeDty...  1.57 us

profile of v5, /device:TPU:1, one launch (start us, length us, event | category | flops | bytes accessed | tf_op | source)
XLA Modules:
  0.0 75.0 jit_solution(1136208889730355085)
XLA Ops:
  0.6 72.8 %adjoint.1 = (f32[3,64,128]{2,1,0:T(8,128)}, f32[64,128]{1,0:T(8,128)}, f32[4,128]{1,0:T(4,128)}) custom-call(f32[4,3,64,128]{3,2,1,0:T(8,128)} %traj_in.1, f32[64,128]{1,0:T(8,128)} %depth_in.1, f32[3,64,128]{2,1,0:T(8,128)} %cot_in.1, f32[64,2048]{1,0:T(8,128)} %line_in.1, f32[128,2048]{1,0:T(8,128)} %column_in.1, s32[1,128]{1,0:T(1,128)} %bitcast.3, ...), custom_call_target="tpu_custom_call" | custom-call | tf_op jit(solution)/shard_map/adjoint/pallas_call | solution.py:732
  73.5 1.6 %hand_over.1 = (f32[3,64,128]{2,1,0:T(8,128)}, f32[64,128]{1,0:T(8,128)}, f32[4,128]{1,0:T(4,128)}) custom-call(f32[3,64,128]{2,1,0:T(8,128)} %get-tuple-element.6.state_in, f32[64,128]{1,0:T(8,128)} %get-tuple-element.7.depth_in, f32[4,128]{1,0:T(4,128)} %get-tuple-element.8.residual_in), custom_call_target="tpu_custom_call" | custom-call | tf_op jit(solution)/shard_map/hand_over/pallas_call | solution.py:757
